TPU v7x, 256 devices: a whole 4x4x8 slice. The times are simulated.
256 devices in a mesh: pair: 8 (over x, z_hi), shard: 32 (over z_lo, y, core).
Axes of the slice: x: 4, y: 4, z: 8 (z_hi: 2, z_lo: 4; z = z_hi * 4 + z_lo), core: 2. Of those that a mesh axis runs over, the one named last changes fastest.
Arguments:
- features: bfloat16 [8, 4096, 1024], P('pair', 'shard'), may hold values from -6 to 6
- w_in: bfloat16 [1024, 1024], P('shard'), may hold values from -0.1875 to 0.1875
- w_out: bfloat16 [1024, 1024], P('shard'), may hold values from -0.1875 to 0.1875
- labels: int32 [8, 4096], P(None, 'shard'), may hold values from 0 to 2047
- pair_list: int32 [512, 2], P('shard'), may hold values from 0 to 7, as said below
Outputs:
- feature_grad: bfloat16 [8, 4096, 1024], P('pair', 'shard')
- in_grad: float32 [1024, 1024], P('shard')
- out_grad: float32 [1024, 1024], P('shard')
- loss: float32 [], replicated
Inputs may be any that keep to these rules, and one draw needn't show every extreme that they name: `pair_list`: within the 16 rows of one batch group no unordered pair repeats, the first entry is never above the second, and a block may be paired with itself.
All inputs are finite; a program needn't handle non-finite values.
Results may differ from a plain program's by a relative error of at most 0.02.
Values may be sent and summed in bfloat16 or wider, within the bound.
A program may use at most 64 MiB of HBM per device.

v0:
```python
import math

import jax
import jax.numpy as jnp
from jax import lax
from jax.sharding import PartitionSpec as P

EPSILON = 1e-06
SIM_SCALE = 10.0
SIM_OFFSET = -5.0
LOSS_SCALE = 256.0


def contract_last(left_array, right_array):
    return lax.dot_general(
        left_array, right_array, (((1,), (1,)), ((), ())), preferred_element_type=jnp.float32
    )


def contract_first(left_array, right_array):
    return lax.dot_general(
        left_array, right_array, (((0,), (0,)), ((), ())), preferred_element_type=jnp.float32
    )


def normalize(vectors):
    feature_width = vectors.shape[-1]
    mean_square = jnp.mean(vectors * vectors, axis=-1, keepdims=True) + EPSILON
    return vectors * (lax.rsqrt(mean_square) / math.sqrt(feature_width))


def normalize_back(vectors, upstream):
    feature_width = vectors.shape[-1]
    mean_square = jnp.mean(vectors * vectors, axis=-1, keepdims=True) + EPSILON
    inverse = lax.rsqrt(mean_square) / math.sqrt(feature_width)
    projected = jnp.sum(upstream * vectors, axis=-1, keepdims=True)
    return inverse * upstream - vectors * (inverse / (feature_width * mean_square)) * projected


def gelu_back(preact, upstream):
    return jax.vjp(jax.nn.gelu, preact)[1](upstream)[0]


def tile_terms(left_block, right_block, left_labels, right_labels):
    scores = contract_last(left_block, right_block)
    logits = SIM_SCALE * scores + SIM_OFFSET
    label_sign = jnp.where(left_labels[:, None] == right_labels[None, :], 1.0, -1.0).astype(
        jnp.float32
    )
    margin = label_sign * logits
    tile_loss = jnp.sum(jax.nn.softplus(-margin))
    tile_slope = (-LOSS_SCALE * SIM_SCALE * label_sign * jax.nn.sigmoid(-margin)).astype(
        jnp.bfloat16
    )
    return (tile_loss, tile_slope)


def given_table(pair_list, owner_count):
    tile_count = pair_list.shape[0]
    owner_ids = jnp.arange(owner_count, dtype=jnp.int32)
    belongs = (pair_list[None, :, 0] == owner_ids[:, None]).astype(jnp.int32)
    ranking = jnp.cumsum(belongs, axis=1) - 1
    slot_ids = jnp.arange(owner_count, dtype=jnp.int32)
    slot_match = (belongs[:, None, :] == 1) & (ranking[:, None, :] == slot_ids[None, :, None])
    tile_ids = jnp.arange(tile_count, dtype=jnp.int32)
    tile_table = jnp.sum(slot_match.astype(jnp.int32) * tile_ids[None, None, :], axis=2)
    tile_valid = jnp.any(slot_match, axis=2)
    return (tile_table, tile_valid, owner_count)


def per_device(features, w_in, w_out, labels, pair_list):
    local_rows = features[0]
    block_size = local_rows.shape[0]
    owner_count = lax.axis_size("pair")
    my_index = lax.axis_index("pair")
    total_rows = owner_count * lax.axis_size("shard") * block_size
    taken = local_rows
    preact = jnp.dot(
        taken, lax.all_gather(w_in, "shard", axis=0, tiled=True), preferred_element_type=jnp.float32
    )
    hidden = jax.nn.gelu(preact).astype(jnp.bfloat16)
    taken = hidden
    embedding = jnp.dot(
        taken,
        lax.all_gather(w_out, "shard", axis=0, tiled=True),
        preferred_element_type=jnp.float32,
    )
    unit_embed = normalize(embedding).astype(jnp.bfloat16)
    width_out = unit_embed.shape[1]
    gathered = lax.all_gather(unit_embed[None], "pair", axis=0, tiled=True)
    tile_table, tile_valid, slot_count = given_table(pair_list, owner_count)
    my_tiles = lax.dynamic_index_in_dim(tile_table, my_index, 0, keepdims=False)
    my_valid = lax.dynamic_index_in_dim(tile_valid, my_index, 0, keepdims=False)

    def tile_parts(tile_index):
        first_block = pair_list[tile_index, 0]
        second = pair_list[tile_index, 1]
        left_block = lax.dynamic_index_in_dim(gathered, first_block, 0, keepdims=False)
        right_block = lax.dynamic_index_in_dim(gathered, second, 0, keepdims=False)
        left_labels = lax.dynamic_index_in_dim(labels, first_block, 0, keepdims=False)
        right_labels = lax.dynamic_index_in_dim(labels, second, 0, keepdims=False)
        tile_loss, tile_slope = tile_terms(left_block, right_block, left_labels, right_labels)
        return (first_block, second, left_block, right_block, tile_loss, tile_slope)

    def visit_blocks(slot_index, carry):
        loss_sum, collected = carry

        def compute(held):
            first_block, second, left_block, right_block, tile_loss, tile_slope = tile_parts(
                my_tiles[slot_index]
            )
            held = held.at[first_block].add(
                jnp.dot(tile_slope, right_block, preferred_element_type=jnp.float32)
            )
            held = held.at[second].add(contract_first(tile_slope, left_block))
            return (tile_loss, held)

        def skip(held):
            return (jnp.zeros((), jnp.float32), held)

        tile_loss, collected = lax.cond(my_valid[slot_index], compute, skip, collected)
        return (loss_sum + tile_loss, collected)

    start_state = (
        jnp.zeros((), jnp.float32),
        jnp.zeros((owner_count, block_size, width_out), jnp.float32),
    )
    loss_sum, collected = lax.fori_loop(0, slot_count, visit_blocks, start_state)
    upstream = lax.psum_scatter(
        collected.astype(jnp.bfloat16), "pair", scatter_dimension=0, tiled=True
    ).astype(jnp.float32)[0]
    embed_grad = normalize_back(embedding, upstream).astype(jnp.bfloat16)
    hidden_grad = contract_last(embed_grad, lax.all_gather(w_out, "shard", axis=0, tiled=True))
    preact_grad = gelu_back(preact, hidden_grad).astype(jnp.bfloat16)
    feature_back = contract_last(preact_grad, lax.all_gather(w_in, "shard", axis=0, tiled=True))
    feature_grad = feature_back.astype(jnp.bfloat16)[None]
    taken = local_rows
    in_share = lax.psum_scatter(
        contract_first(taken, preact_grad).astype(jnp.bfloat16),
        "shard",
        scatter_dimension=0,
        tiled=True,
    )
    taken = hidden
    out_share = lax.psum_scatter(
        contract_first(taken, embed_grad).astype(jnp.bfloat16),
        "shard",
        scatter_dimension=0,
        tiled=True,
    )
    in_total, out_total = (
        lax.psum(in_share, "pair").astype(jnp.float32),
        lax.psum(out_share, "pair").astype(jnp.float32),
    )
    factor = 1.0 / math.sqrt(total_rows)
    loss = lax.psum(loss_sum, ("pair", "shard")) / total_rows
    return (feature_grad, in_total * factor, out_total * factor, loss)


def solution(mesh):
    in_specs = (
        P("pair", "shard", None),
        P("shard", None),
        P("shard", None),
        P(None, "shard"),
        P("shard", None),
    )
    out_specs = (P("pair", "shard", None), P("shard", None), P("shard", None), P())
    return jax.shard_map(
        per_device, mesh=mesh, in_specs=in_specs, out_specs=out_specs, check_vma=False
    )
```

profile of v0, /device:TPU:1, one launch (start us, length us, event | category | flops | bytes accessed | tf_op | source)
XLA Modules:
  0.0 822.8 jit_solution(12566352650978125043)
XLA Ops:
  8.7 65.5 %all-gather.5.cloned.1.call-done = bf16[1024,1024]{1,0:T(8,128)(2,1)} async-done(((bf16[32,1024]{1,0:T(8,128)(2,1)}), bf16[1024,1024]{1,0:T(8,128)(2,1)}) %all-gather.5.cloned.1.call-update) | async-done | bytes 2097168 | tf_op jit(solution)/shard_map/all_gather | solution.py:79
  76.3 58.9 %all-gather.7.cloned.1.call-done = bf16[1024,1024]{1,0:T(8,128)(2,1)} async-done(((bf16[32,1024]{1,0:T(8,128)(2,1)}), bf16[1024,1024]{1,0:T(8,128)(2,1)}) %all-gather.7.cloned.1.call-update) | async-done | bytes 2097168 | tf_op jit(solution)/shard_map/all_gather | solution.py:85
  139.0 72.8 %all-gather.9.cloned.1.call-done = bf16[1024,1024]{1,0:T(8,128)(2,1)} async-done(((bf16[128,1024]{1,0:T(8,128)(2,1)}), bf16[1024,1024]{1,0:T(8,128)(2,1)}) %all-gather.9.cloned.1.call-update) | async-done | bytes 2097168 | tf_op jit(solution)/shard_map/all_gather | solution.py:90
  214.3 74.4 %while.20 = (s32[]{:T(128)}, f32[]{:T(128)}, f32[8,128,1024]{2,1,0:T(8,128)}, pred[8]{0:T(512)(128)(4,1)S(1)}, s32[8]{0:T(128)S(1)}, /*index=5*/s32[16,2]{0,1:T(...) while((s32[]{:T(128)}, f32[]{:T(128)}, f32[8,128,1024]{2,1,0:T(8,128)}, ...), condition=%wide.region_10.11_spmd, body=%wide.region_4.10_spmd.sunk | while | flops 101630000 | bytes 3350922 | solution.py:128
  215.5 16.1 %conditional.2 = (f32[]{:T(128)}, f32[8,128,1024]{2,1,0:T(8,128)}) conditional(s32[]{:T(128)} %bitcast.71, f32[8,128,1024]{2,1,0:T(8,128)} %get-tuple-element.307, (s32[]{:T(128)}, s32[8]{0:T(128)S(1)}, s32[16,2]{0,1:T(2,128)S(1)}, s32[8,128]{1,0:T(8,128)}, bf16[8,128,1024]{2,1,0:T(8,128)(2,1)S(1)}, /*index=5*/f32[8,128,1024]{2,1,0:T(8,128)}) %tuple.64), branch_computations={%region_5.5_spmd, %region_6.9_spmd} | conditional | flops 101630000 | bytes 3350758 | solution.py:121
  225.5 2.6 fusion.2
  228.1 2.8 fusion.5
  232.8 16.1 %conditional.2 = (f32[]{:T(128)}, f32[8,128,1024]{2,1,0:T(8,128)}) conditional(s32[]{:T(128)} %bitcast.71, f32[8,128,1024]{2,1,0:T(8,128)} %get-tuple-element.307, (s32[]{:T(128)}, s32[8]{0:T(128)S(1)}, s32[16,2]{0,1:T(2,128)S(1)}, s32[8,128]{1,0:T(8,128)}, bf16[8,128,1024]{2,1,0:T(8,128)(2,1)S(1)}, /*index=5*/f32[8,128,1024]{2,1,0:T(8,128)}) %tuple.64), branch_computations={%region_5.5_spmd, %region_6.9_spmd} | conditional | flops 101630000 | bytes 3350758 | solution.py:121
  242.8 2.6 fusion.2
  245.5 2.8 fusion.5
  250.2 16.1 %conditional.2 = (f32[]{:T(128)}, f32[8,128,1024]{2,1,0:T(8,128)}) conditional(s32[]{:T(128)} %bitcast.71, f32[8,128,1024]{2,1,0:T(8,128)} %get-tuple-element.307, (s32[]{:T(128)}, s32[8]{0:T(128)S(1)}, s32[16,2]{0,1:T(2,128)S(1)}, s32[8,128]{1,0:T(8,128)}, bf16[8,128,1024]{2,1,0:T(8,128)(2,1)S(1)}, /*index=5*/f32[8,128,1024]{2,1,0:T(8,128)}) %tuple.64), branch_computations={%region_5.5_spmd, %region_6.9_spmd} | conditional | flops 101630000 | bytes 3350758 | solution.py:121
  260.1 2.6 fusion.2
  262.8 2.8 fusion.5
  267.5 16.1 %conditional.2 = (f32[]{:T(128)}, f32[8,128,1024]{2,1,0:T(8,128)}) conditional(s32[]{:T(128)} %bitcast.71, f32[8,128,1024]{2,1,0:T(8,128)} %get-tuple-element.307, (s32[]{:T(128)}, s32[8]{0:T(128)S(1)}, s32[16,2]{0,1:T(2,128)S(1)}, s32[8,128]{1,0:T(8,128)}, bf16[8,128,1024]{2,1,0:T(8,128)(2,1)S(1)}, /*index=5*/f32[8,128,1024]{2,1,0:T(8,128)}) %tuple.64), branch_computations={%region_5.5_spmd, %region_6.9_spmd} | conditional | flops 101630000 | bytes 3350758 | solution.py:121
  277.5 2.6 fusion.2
  280.1 2.8 fusion.5
  288.7 3.9 convert_element_type.62
  292.7 119.3 %reduce-scatter.8.cloned.1.call-done = bf16[1,128,1024]{2,1,0:T(8,128)(2,1)} async-done(((bf16[8,128,1024]{2,1,0:T(8,128)(2,1)}), bf16[1,128,1024]{2,1,0:T(8,128)(2,1)}) %reduce-scatter.8.cloned.1.call-update) | async-done | bytes 262160 | tf_op jit(solution)/shard_map/reduce_scatter | solution.py:129
  413.0 3.2 convolution_convert_fusion
  419.7 2.6 copy.18
  422.4 76.5 %psum.23 = f32[]{:T(128)} all-reduce(f32[]{:T(128)} %get-tuple-element.192), channel_id=1, replica_groups=mesh['pair'=8,'shard'=32] {'pair','shard'}, use_global_device_ids=true, to_apply=%region_17.18 | all-reduce | flops 1 | bytes 8 | tf_op jit(solution)/shard_map/psum | solution.py:156
  499.5 55.8 %reduce-scatter.12.cloned.1.call-done = bf16[32,1024]{1,0:T(8,128)(2,1)} async-done(((bf16[1024,1024]{1,0:T(8,128)(2,1)}), bf16[32,1024]{1,0:T(8,128)(2,1)}) %reduce-scatter.12.cloned.1.call-update) | async-done | bytes 65552
  557.0 143.7 %reduce-scatter.10.cloned.1.call-done = bf16[32,1024]{1,0:T(8,128)(2,1)} async-done(((bf16[1024,1024]{1,0:T(8,128)(2,1)}), bf16[32,1024]{1,0:T(8,128)(2,1)}) %reduce-scatter.10.cloned.1.call-update) | async-done | bytes 65552
  704.0 108.1 %all-reduce.3.cloned.1.call-done = (bf16[32,1024]{0,1:T(8,128)(2,1)}, bf16[32,1024]{0,1:T(8,128)(2,1)}) async-done(((bf16[32,1024]{0,1:T(8,128)(2,1)}, bf16[32,1024]{0,1:T(8,128)(2,1)}), (bf16[32,1024]{0,1:T(8,128)(2,1)}, bf16[32,1024]{0,1:T(8,128)(2,1)})) %all-reduce.3.cloned.1.call-update) | async-done | bytes 131088 | tf_op jit(solution)/shard_map/psum | solution.py:152
  (78 shorter events, 43.5 us)
Async XLA Ops:
  7.2 67.1 %copy-start = (bf16[1,128,1024]{2,1,0:T(8,128)(2,1)S(1)}, bf16[1,128,1024]{2,1,0:T(8,128)(2,1)}, u32[]{:S(2)}) copy-start(bf16[1,128,1024]{2,1,0:T(8,128)(2,1)} %param.13) | copy-start | bytes 786436
  7.2 67.1 %all-gather.5.cloned.1.call-start = ((), (), s32[]{:S(2)}) async-start(), calls=%async_computation.3 | async-start | bytes 2162688 | tf_op jit(solution)/shard_map/all_gather | solution.py:79
  7.9 127.3 %all-gather.7.cloned.1.call-start = ((), (), s32[]{:S(2)}) async-start(), calls=%async_computation.4 | async-start | bytes 2162688 | tf_op jit(solution)/shard_map/all_gather | solution.py:85
  8.7 203.1 %all-gather.9.cloned.1.call-start = ((), (), s32[]{:S(2)}) async-start(), calls=%async_computation.6 | async-start | bytes 2359296 | tf_op jit(solution)/shard_map/all_gather | solution.py:90
  76.3 62.0 %copy-start.4 = (s32[16,2]{0,1:T(2,128)S(1)}, s32[16,2]{0,1:T(2,128)}, u32[]{:S(2)}) copy-start(s32[16,2]{0,1:T(2,128)} %param.17) | copy-start | bytes 388
  138.2 273.7 %reduce-scatter.8.cloned.1.call-start = ((), (), s32[]{:S(2)}) async-start(), calls=%async_computation.5 | async-start | bytes 2359296 | tf_op jit(solution)/shard_map/reduce_scatter | solution.py:129
  211.8 2.5 copy-start.2
  292.6 262.7 %reduce-scatter.12.cloned.1.call-start = ((), (), s32[]{:S(2)}) async-start(), calls=%async_computation.8 | async-start | bytes 2162688
  413.0 3.3 copy-start.3
  416.3 284.5 %reduce-scatter.10.cloned.1.call-start = ((), (), s32[]{:S(2)}) async-start(), calls=%async_computation.7 | async-start | bytes 2162688
  422.3 280.1 %copy-start.1 = (bf16[1024,1024]{1,0:T(8,128)(2,1)S(1)}, bf16[1024,1024]{1,0:T(8,128)(2,1)}, u32[]{:S(2)}) copy-start(bf16[1024,1024]{1,0:T(8,128)(2,1)} %all-gather.5.cloned.1.call-done) | copy-start | bytes 6291460
  422.4 389.7 %all-reduce.3.cloned.1.call-start = ((), (), s32[]{:S(2)}) async-start(), calls=%async_computation.9 | async-start | bytes 1048576 | tf_op jit(solution)/shard_map/psum | solution.py:152
Sparse Core Ops, SparseCore 0:
  9.9 64.3 all-gather.4
  76.1 59.0 all-gather.6
  138.4 73.3 all-gather.8
  292.8 119.1 reduce-scatter.7
  416.4 138.8 reduce-scatter.11
  557.7 142.9 reduce-scatter.9
  703.6 108.3 all-reduce.2
where the time goes:
time: 830 us; the launch traced here: 823 us
  waiting for transfers between devices  626 us (75%)
  blocking collectives  76.5 us (9%)
  matrix products  37.6 us (5%)
  loops' own time  31.2 us (4%)
  local copies, waits for them, and re-layouts  22.7 us (3%)
  between operations  16 us (2%)
  other arithmetic  13.1 us (2%)
    unnamed x9, waiting for transfers between devices  201 us
    reduce_scatter x1, waiting for transfers between devices, per_device(): lax.psum_scatter(collected.astype(jnp.bfloat16), 'pair', scatter_dimensio...  119 us
    psum x1, waiting for transfers between devices, per_device(): lax.psum(in_share, 'pair').astype(jnp.float32)  108 us
    psum x1, blocking collectives, per_device(): loss = lax.psum(loss_sum, ('pair', 'shard')) / total_rows  76.5 us
    all_gather x1, waiting for transfers between devices, per_device(): gathered = lax.all_gather(unit_embed[None], 'pair', axis=0, tiled=True)  72.8 us
    all_gather x1, waiting for transfers between devices, per_device(): lax.all_gather(w_in, 'shard', axis=0, tiled=True)  65.5 us
    all_gather x1, waiting for transfers between devices, per_device(): lax.all_gather(w_out, 'shard', axis=0, tiled=True)  58.9 us
    another operation x8, loops' own time, visit_blocks(): lax.cond(my_valid[slot_index], compute, skip, collected)  25.7 us
  transfers between devices with their start and end apart: 7, of which 7 were waited for; matrix products, arithmetic and copies ran while one was open for 1% of the time, Pallas kernels for 0%

commit v1 on v0

v1 whole, which is shorter than its diff:
```python
import functools
import math

import jax
import jax.numpy as jnp
from jax import lax
from jax.experimental import pallas as pl
from jax.experimental.pallas import tpu as pltpu
from jax.sharding import PartitionSpec as P

MESH = pl.DeviceIdType.MESH
BF16 = jnp.bfloat16
F32 = jnp.float32

EPSILON = 1e-06
SIM_SCALE = 10.0
SIM_OFFSET = -5.0
LOSS_SCALE = 256.0
WIDTH = 1024
GELU_A = math.sqrt(2.0 / math.pi)
GELU_B = 0.044715
COPIES = 128


def dot_nn(a, b):
    return lax.dot_general(a, b, (((1,), (0,)), ((), ())), preferred_element_type=F32)


def dot_nt(a, b):
    return lax.dot_general(a, b, (((1,), (1,)), ((), ())), preferred_element_type=F32)


def gelu(v):
    return 0.5 * v * (1.0 + jnp.tanh(GELU_A * (v + GELU_B * v * v * v)))


def gelu_slope(v):
    t = jnp.tanh(GELU_A * (v + GELU_B * v * v * v))
    inner = GELU_A * (1.0 + 3.0 * GELU_B * v * v)
    return 0.5 * (1.0 + t) + 0.5 * v * (1.0 - t * t) * inner


def tile_at(n, size):
    return pl.ds(pl.multiple_of(n * size, size), size)


def kernel(
    total_rows,
    feat,
    w_in,
    w_out,
    labels,
    pairs,
    fg_out,
    ig_out,
    og_out,
    loss_out,
    fx,
    wi,
    wo,
    pre,
    hid,
    emb,
    uni,
    slope,
    ups,
    eg2,
    pg2,
    tr,
    lt,
    gs_in,
    gs_out,
    r1_in,
    r1_out,
    s1_in,
    s1_out,
    r2,
    s2,
    r3,
    s3,
    r4,
    s4,
    ag,
    lk,
    ly,
    lx,
    lz,
    lz2,
    ssem,
    rsem,
    lsem,
):
    pair = lax.axis_index("pair")
    shard = lax.axis_index("shard")
    x, zh = pair // 2, pair % 2
    zl, y, k = shard // 8, (shard // 2) % 4, shard % 2
    z = zh * 4 + zl

    def device(dx=0, dy=0, dz=0, dk=0):
        zz = (z + dz + 8) % 8
        return (
            ((x + dx + 4) % 4) * 2 + zz // 4,
            (zz % 4) * 8 + ((y + dy + 4) % 4) * 2 + (k + dk) % 2,
        )

    started = []

    def send(src, dst, **offset):
        i = len(started)
        copy = pltpu.make_async_remote_copy(
            src_ref=src,
            dst_ref=dst,
            send_sem=ssem.at[i],
            recv_sem=rsem.at[i],
            device_id=device(**offset),
            device_id_type=MESH,
        )
        copy.start()
        started.append(copy)
        return copy

    barrier = pltpu.get_barrier_semaphore()
    partners = (
        [dict(dx=d) for d in (1, -1, 2)]
        + [dict(dy=d) for d in (1, -1, 2)]
        + [dict(dz=d) for d in (1, -1, 2, -2, 4)]
        + [dict(dk=1)]
    )
    for offset in partners:
        pl.semaphore_signal(barrier, inc=1, device_id=device(**offset), device_id_type=MESH)
    lz[...] = jnp.zeros_like(lz)
    pl.semaphore_wait(barrier, len(partners))

    weights = ((w_in, wi), (w_out, wo))
    zl_of = (zl, (zl + 3) % 4, (zl + 1) % 4, (zl + 2) % 4)

    z_copies = []
    for src, dst in weights:
        z_copies.append(
            (
                [send(src, dst.at[zl, y, k], dz=1)],
                [send(src, dst.at[zl, y, k], dz=-1)],
                [
                    send(src.at[pl.ds(0, 16)], dst.at[zl, y, k, pl.ds(0, 16)], dz=2),
                    send(src.at[pl.ds(16, 16)], dst.at[zl, y, k, pl.ds(16, 16)], dz=-2),
                ],
            )
        )
    y_copies = [[], []]
    for t, (src, dst) in enumerate(weights):
        y_copies[t].append([send(src, dst.at[zl, y, k], dy=d) for d in (1, -1, 2)])
    f_z = send(feat, fx.at[zh, x], dz=4)
    f_x = [send(feat, fx.at[zh, x], dx=d) for d in (1, -1, 2)]

    fx[zh, x] = feat[...]
    wi[zl, y, k] = w_in[...]
    wo[zl, y, k] = w_out[...]

    def transpose_to(t, read):
        for n in range(8):
            block = read(n).T
            for i in range(4):
                s = n * 4 + i
                tr[t, s // 2, s % 2] = block[i * 32 : i * 32 + 32]
        local = pltpu.make_async_copy(
            tr.at[t, :, k], lt.at[t, :, :, pl.ds(0, 128)], lsem.at[t]
        )
        local.start()
        return local, send(tr.at[t, :, 1 - k], lt.at[t, :, :, pl.ds(128, 128)], dk=1)

    def y_stage(t, j):
        buf = weights[t][1]
        for copy in z_copies[t][j - 1]:
            copy.wait_recv()
        block = buf.at[zl_of[j], y, k]
        y_copies[t].append([send(block, block, dy=d) for d in (1, -1, 2)])

    def core_stage(t, j):
        buf = weights[t][1]
        for copy in y_copies[t][j]:
            copy.wait_recv()
        half = buf.at[zl_of[j], :, k]
        return send(half, half, dk=1)

    for j in (1, 2, 3):
        y_stage(0, j)
    for j in (1, 2, 3):
        y_stage(1, j)
    f_local, f_core = transpose_to(0, lambda n: feat[:, n * 128 : n * 128 + 128])
    f_z.wait_recv()
    block = fx.at[1 - zh, x]
    f_xz = [send(block, block, dx=d) for d in (1, -1, 2)]

    in_core = [core_stage(0, j) for j in range(4)]
    for copy in in_core:
        copy.wait_recv()
    for copy in f_x:
        copy.wait_recv()

    def hidden_of(group, keep):
        def step(n, carry):
            cols = tile_at(n, 256)
            acc = dot_nn(
                fx[group].reshape(512, WIDTH), wi[:, :, :, :, cols].reshape(WIDTH, 256)
            )
            if keep:
                pre[:, cols] = acc
            hid[group, :, cols] = gelu(acc).astype(BF16)
            return carry

        lax.fori_loop(0, 4, step, 0)

    def embed_of(group):
        def step(n, carry):
            cols = tile_at(n, 256)
            emb[group, :, cols] = dot_nn(hid[group], wo[:, :, :, :, cols].reshape(WIDTH, 256))
            return carry

        lax.fori_loop(0, 4, step, 0)

        def norm(n, carry):
            rows = tile_at(n, 64)
            v = emb[group, rows, :]
            mean_square = jnp.mean(v * v, axis=-1, keepdims=True) + EPSILON
            uni[group, rows, :] = (v * (lax.rsqrt(mean_square) / math.sqrt(WIDTH))).astype(BF16)
            return carry

        lax.fori_loop(0, 8, norm, 0)

    hidden_of(zh, True)
    own = tile_at(x, 128)
    h_local, h_core = transpose_to(1, lambda n: hid[zh, own, n * 128 : n * 128 + 128])

    for copy in f_xz:
        copy.wait_recv()
    hidden_of(1 - zh, False)
    out_core = [core_stage(1, j) for j in range(4)]
    for copy in out_core:
        copy.wait_recv()
    embed_of(zh)
    embed_of(1 - zh)

    codes = [pairs[i, 0] * 8 + pairs[i, 1] for i in range(16)]
    own_labels = jnp.broadcast_to(labels[pl.ds(pair, 1), :].astype(F32), (128, 128)).T
    loss_sum = jnp.zeros((128, 128), F32)
    for g in range(2):
        scores = dot_nt(uni[zh, own, :], uni[g])
        for i in range(4):
            q = i * 2 + g
            target = jnp.minimum(pair, q) * 8 + jnp.maximum(pair, q)
            listed = functools.reduce(
                lambda a, b: a + b, [jnp.where(c == target, 1.0, 0.0) for c in codes]
            )
            twice = jnp.where(pair == q, 2.0, 1.0)
            counted = jnp.where(pair <= q, 1.0, 0.0)
            logits = SIM_SCALE * scores[:, i * 128 : i * 128 + 128] + SIM_OFFSET
            same = own_labels == labels[q : q + 1, :].astype(F32)
            sign = jnp.where(same, 1.0, -1.0)
            margin = sign * logits
            small = jnp.exp(-jnp.abs(margin))
            loss_sum += (listed * counted) * (jnp.maximum(-margin, 0.0) + jnp.log1p(small))
            share = jnp.where(margin >= 0.0, small, 1.0) / (1.0 + small)
            slope[:, g * 512 + i * 128 : g * 512 + i * 128 + 128] = (
                (-LOSS_SCALE * SIM_SCALE * sign * share).astype(BF16).astype(F32)
                * (listed * twice)
            ).astype(BF16)
    loss_total = jnp.broadcast_to(
        jnp.sum(jnp.sum(loss_sum, axis=0, keepdims=True), axis=1, keepdims=True), (8, 128)
    )
    lk[k] = loss_total
    loss_core = send(lk.at[k], lk.at[k], dk=1)

    def upstream(n, carry):
        cols = tile_at(n, 256)
        ups[:, cols] = dot_nn(slope[...], uni[:, :, cols].reshape(WIDTH, 256))
        return carry

    lax.fori_loop(0, 4, upstream, 0)

    def embed_back(n, carry):
        rows = tile_at(n, 32)
        v = emb[zh, pl.ds(pl.multiple_of(x * 128 + n * 32, 32), 32), :]
        up = ups[rows, :]
        mean_square = jnp.mean(v * v, axis=-1, keepdims=True) + EPSILON
        inverse = lax.rsqrt(mean_square) / math.sqrt(WIDTH)
        projected = jnp.sum(up * v, axis=-1, keepdims=True)
        grad = inverse * up - v * (inverse / (WIDTH * mean_square)) * projected
        eg2[rows, :] = grad.astype(BF16)
        return carry

    lax.fori_loop(0, 4, embed_back, 0)
    eg_core = send(eg2.at[pl.ds(0, 128)], eg2.at[pl.ds(128, 128)], dk=1)

    def hidden_back(n, carry):
        cols = tile_at(n, 256)
        hidden_grad = dot_nt(eg2[pl.ds(0, 128), :], wo[n].reshape(256, WIDTH))
        pg2[pl.ds(0, 128), cols] = (hidden_grad * gelu_slope(pre[own, cols])).astype(BF16)
        return carry

    lax.fori_loop(0, 4, hidden_back, 0)
    pg_core = send(pg2.at[pl.ds(0, 128)], pg2.at[pl.ds(128, 128)], dk=1)

    def weight_grad(t, rows_ref, dst):
        def step(n, carry):
            cols = tile_at(n, 256)
            grad = dot_nn(lt[t].reshape(512, 256), rows_ref[:, cols])
            dst[:, :, :, cols] = grad.astype(BF16).reshape(4, 4, 32, 256)
            return carry

        lax.fori_loop(0, 4, step, 0)

    h_local.wait()
    h_core.wait_recv()
    eg_core.wait_recv()
    weight_grad(1, eg2, gs_out)
    out_1 = [
        send(gs_out.at[:, (y + d + 4) % 4], r1_out.at[i], dy=d) for i, d in enumerate((1, -1, 2))
    ]
    loss_core.wait_recv()
    ly[y] = lk[0] + lk[1]
    loss_y = [send(ly.at[y], ly.at[y], dy=d) for d in (1, -1, 2)]
    f_local.wait()
    f_core.wait_recv()
    pg_core.wait_recv()
    weight_grad(0, pg2, gs_in)
    in_1 = [
        send(gs_in.at[:, :, :, tile_at((x + d + 4) % 4, 256)], r1_in.at[i], dx=d)
        for i, d in enumerate((1, -1, 2))
    ]

    def feature_back(n, carry):
        cols = tile_at(n, 256)
        fg_out[:, cols] = dot_nt(pg2[pl.ds(0, 128), :], wi[n].reshape(256, WIDTH)).astype(BF16)
        return carry

    lax.fori_loop(0, 4, feature_back, 0)

    for copy in out_1:
        copy.wait_recv()
    for i in range(4):
        total = gs_out[i, y].astype(F32)
        for j in range(3):
            total += r1_out[j, i].astype(F32)
        s1_out[i] = total.astype(BF16)
    out_2 = [
        send(s1_out.at[:, :, tile_at((x + d + 4) % 4, 256)], r2.at[1, i], dx=d)
        for i, d in enumerate((1, -1, 2))
    ]
    for copy in loss_y:
        copy.wait_recv()
    lx[x] = (ly[0] + ly[1]) + (ly[2] + ly[3])
    loss_x = [send(lx.at[x], lx.at[x], dx=d) for d in (1, -1, 2)]

    for copy in in_1:
        copy.wait_recv()
    for i in range(4):
        total = gs_in[i, :, :, tile_at(x, 256)].astype(F32)
        for j in range(3):
            total += r1_in[j, i].astype(F32)
        s1_in[i] = total.astype(BF16)
    in_2 = [
        send(s1_in.at[:, (y + d + 4) % 4], r2.at[0, i], dy=d) for i, d in enumerate((1, -1, 2))
    ]

    def z_stage(t, mine, copies):
        for copy in copies:
            copy.wait_recv()
        total = mine().astype(F32)
        for j in range(3):
            total += r2[t, j].astype(F32)
        s2[t] = total.astype(BF16)
        far = s2.at[t, (zl + 2) % 4]
        return [
            send(s2.at[t, (zl + 1) % 4], r3.at[t, 0], dz=1),
            send(s2.at[t, (zl + 3) % 4], r3.at[t, 1], dz=-1),
            send(far.at[pl.ds(0, 16)], r3.at[t, 2, pl.ds(0, 16)], dz=2),
            send(far.at[pl.ds(16, 16)], r3.at[t, 2, pl.ds(16, 16)], dz=-2),
        ]

    out_3 = z_stage(1, lambda: s1_out[:, :, tile_at(x, 256)], out_2)
    for copy in loss_x:
        copy.wait_recv()
    lz[z] = (lx[0] + lx[1]) + (lx[2] + lx[3])
    loss_z = [send(lz.at[z], lz.at[z], dz=d) for d in (1, -1, 2, -2)]
    in_3 = z_stage(0, lambda: s1_in[:, y], in_2)

    def far_stage(t, copies):
        for copy in copies:
            copy.wait_recv()
        total = s2[t, zl].astype(F32)
        for j in range(3):
            total += r3[t, j].astype(F32)
        s3[t] = total.astype(BF16)
        return send(s3.at[t], r4.at[t], dz=4)

    out_4 = far_stage(1, out_3)
    for copy in loss_z:
        copy.wait_recv()
    loss_far = send(lz, lz2, dz=4)
    in_4 = far_stage(0, in_3)

    def spread(t, copy):
        copy.wait_recv()
        s4[t] = (s3[t].astype(F32) + r4[t].astype(F32)).astype(BF16)
        cols = tile_at(x, 256)
        copies = [send(s4.at[t], ag.at[t, :, cols], dx=d) for d in (1, -1, 2)]
        ag[t, :, cols] = s4[t]
        return copies

    out_5 = spread(1, out_4)
    in_5 = spread(0, in_4)

    loss_far.wait_recv()
    loss = jnp.zeros((8, 128), F32)
    for i in range(8):
        away = (i - z + 8) % 8
        near = jnp.where(away <= 2, 1, jnp.where(away >= 6, 1, 0))
        loss += jnp.where(near == 1, lz[i], lz2[i])
    loss_out[...] = loss / total_rows

    factor = 1.0 / math.sqrt(total_rows)
    for copy in out_5:
        copy.wait_recv()
    og_out[...] = ag[1].astype(F32) * factor
    for copy in in_5:
        copy.wait_recv()
    ig_out[...] = ag[0].astype(F32) * factor
    for copy in started:
        copy.wait_send()


def per_device(features, w_in, w_out, labels, pair_list):
    total_rows = lax.axis_size("pair") * lax.axis_size("shard") * features.shape[1]
    vmem = pl.BlockSpec(memory_space=pltpu.VMEM)
    smem = pl.BlockSpec(memory_space=pltpu.SMEM)
    w = WIDTH
    fg, ig, og, loss = pl.pallas_call(
        functools.partial(kernel, total_rows),
        name="contrastive_step",
        out_shape=(
            jax.ShapeDtypeStruct((128, w), BF16),
            jax.ShapeDtypeStruct((32, w), F32),
            jax.ShapeDtypeStruct((32, w), F32),
            jax.ShapeDtypeStruct((8, 128), F32),
        ),
        in_specs=[vmem, vmem, vmem, vmem, smem],
        out_specs=(vmem, vmem, vmem, vmem),
        scratch_shapes=[
            pltpu.VMEM((2, 4, 128, w), BF16),
            pltpu.VMEM((4, 4, 2, 32, w), BF16),
            pltpu.VMEM((4, 4, 2, 32, w), BF16),
            pltpu.VMEM((512, w), F32),
            pltpu.VMEM((2, 512, w), BF16),
            pltpu.VMEM((2, 512, w), F32),
            pltpu.VMEM((2, 512, w), BF16),
            pltpu.VMEM((128, w), BF16),
            pltpu.VMEM((128, w), F32),
            pltpu.VMEM((256, w), BF16),
            pltpu.VMEM((256, w), BF16),
            pltpu.VMEM((2, 16, 2, 32, 128), BF16),
            pltpu.VMEM((2, 16, 32, 256), BF16),
            pltpu.VMEM((4, 4, 32, w), BF16),
            pltpu.VMEM((4, 4, 32, w), BF16),
            pltpu.VMEM((3, 4, 4, 32, 256), BF16),
            pltpu.VMEM((3, 4, 32, w), BF16),
            pltpu.VMEM((4, 4, 32, 256), BF16),
            pltpu.VMEM((4, 32, w), BF16),
            pltpu.VMEM((2, 3, 4, 32, 256), BF16),
            pltpu.VMEM((2, 4, 32, 256), BF16),
            pltpu.VMEM((2, 3, 32, 256), BF16),
            pltpu.VMEM((2, 32, 256), BF16),
            pltpu.VMEM((2, 32, 256), BF16),
            pltpu.VMEM((2, 32, 256), BF16),
            pltpu.VMEM((2, 32, w), BF16),
            pltpu.VMEM((2, 8, 128), F32),
            pltpu.VMEM((4, 8, 128), F32),
            pltpu.VMEM((4, 8, 128), F32),
            pltpu.VMEM((8, 8, 128), F32),
            pltpu.VMEM((8, 8, 128), F32),
            pltpu.SemaphoreType.DMA((COPIES,)),
            pltpu.SemaphoreType.DMA((COPIES,)),
            pltpu.SemaphoreType.DMA((2,)),
        ],
        compiler_params=pltpu.CompilerParams(
            collective_id=0, has_side_effects=True, vmem_limit_bytes=48 * 2**20
        ),
    )(features[0], w_in, w_out, labels, pair_list)
    return fg[None], ig, og, loss[0, 0]


def solution(mesh):
    in_specs = (
        P("pair", "shard", None),
        P("shard", None),
        P("shard", None),
        P(None, "shard"),
        P("shard", None),
    )
    out_specs = (P("pair", "shard", None), P("shard", None), P("shard", None), P())
    return jax.shard_map(
        per_device, mesh=mesh, in_specs=in_specs, out_specs=out_specs, check_vma=False
    )
```

time: 830 us -> 99.5 us (0.12)
  waiting for transfers between devices: 626 us -> 0 us
  Pallas kernels: 0 us -> 90.5 us
  blocking collectives: 76.5 us -> 0 us
  matrix products: 37.6 us -> 0 us
  loops' own time: 31.2 us -> 0 us
  local copies, waits for them, and re-layouts: 22.7 us -> 6.51 us
  between operations: 16 us -> 0.65 us
  other arithmetic: 13.1 us -> 0 us
    unnamed x9 -> x0, waiting for transfers between devices: 201 us -> none
    all_gather x3 -> x0, waiting for transfers between devices: 197 us -> none  [the longest x1 72.8 us: per_device(): gathered = lax.all_gather(unit_embed[None], 'pair', axis=0, tiled=True)]
    reduce_scatter x1 -> x0, waiting for transfers between devices: 119 us -> none  [per_device(): lax.psum_scatter(collected.astype(jnp.bfloat16), 'pair', scatter_dimensio...]
    psum x1 -> x0, waiting for transfers between devices: 108 us -> none  [per_device(): lax.psum(in_share, 'pair').astype(jnp.float32)]
    pallas_call x0 -> x1, Pallas kernels: none -> 90.5 us  [per_device(): pl.pallas_call(functools.partial(kernel, total_rows), name='contrastive_s...]
    psum x1 -> x0, blocking collectives: 76.5 us -> none  [per_device(): loss = lax.psum(loss_sum, ('pair', 'shard')) / total_rows]
    dot_general x18 -> x0, matrix products: 37.6 us -> none  [the longest x6 15.2 us: contract_first(): lax.dot_general(left_array, right_array, (((0,), (0,)), ((), ())), prefer...]
    another operation x9 -> x0, loops' own time: 31.2 us -> none  [the longest x8 25.7 us: visit_blocks(): lax.cond(my_valid[slot_index], compute, skip, collected)]
  transfers between devices with their start and end apart: 7 -> 0, of which waited for: 7 -> 0; matrix products, arithmetic and copies ran while one was open for 1% -> 0% of each run, Pallas kernels for 0% -> 0%
where the time goes in v1:
time: 99.5 us; the launch traced here: 97.7 us
  Pallas kernels  90.5 us (91%)
  local copies, waits for them, and re-layouts  6.51 us (7%)
    pallas_call x1, Pallas kernels, per_device(): pl.pallas_call(functools.partial(kernel, total_rows), name='contrastive_s...  90.5 us
    unnamed x14, local copies, waits for them, and re-layouts  6 us

profile of v1, /device:TPU:1, one launch (start us, length us, event | category | flops | bytes accessed | tf_op | source)
XLA Modules:
  0.0 97.7 jit_solution(8552898295955464759)
XLA Ops:
  0.6 0.0 copy-start.4
  0.6 0.7 copy-done.4
  1.3 0.0 copy-start.3
  1.3 0.1 copy.9.pairs
  1.4 0.6 copy-done.3
  2.0 0.0 copy-start
  2.0 0.9 copy-done
  2.9 0.0 copy-start.1
  3.0 0.8 copy-done.1
  3.8 0.0 copy-start.2
  3.8 0.8 copy-done.2
  4.6 90.5 %contrastive_step.1 = (bf16[128,1024]{1,0:T(8,128)(2,1)S(1)}, f32[32,1024]{1,0:T(8,128)S(1)}, f32[32,1024]{1,0:T(8,128)S(1)}, f32[8,128]{1,0:T(8,128)S(1)}) custom-call(bf16[128,1024]{1,0:T(8,128)(2,1)S(1)} %bitcast.3, bf16[32,1024]{1,0:T(8,128)(2,1)S(1)} %copy-done.1, bf16[32,1024]{1,0:T(8,128)(2,1)S(1)} %copy-done.2, s32[8,128]{1,0:T(8,128)S(1)} %copy-done.3, ...), custom_call_target="tpu_custom_call" | custom-call | tf_op jit(solution)/shard_map/contrastive_step/pallas_call | solution.py:437
  95.1 0.5 slice.3
  95.6 0.7 copy.13
  96.3 0.7 copy.14
  97.0 0.7 copy.15
Async XLA Ops:
  0.6 0.7 copy-start.4
  1.3 0.7 copy-start.3
  2.0 0.9 copy-start
  2.9 0.8 copy-start.1
  3.8 0.8 copy-start.2

commit v2 on v1

v2 whole, which is shorter than its diff:
```python
import functools
import math

import jax
import jax.numpy as jnp
from jax import lax
from jax.experimental import pallas as pl
from jax.experimental.pallas import tpu as pltpu
from jax.sharding import PartitionSpec as P

MESH = pl.DeviceIdType.MESH
BF16 = jnp.bfloat16
F32 = jnp.float32

EPSILON = 1e-06
SIM_SCALE = 10.0
SIM_OFFSET = -5.0
LOSS_SCALE = 256.0
WIDTH = 1024
GELU_A = math.sqrt(2.0 / math.pi)
GELU_B = 0.044715
COPIES = 160


def dot_nn(a, b):
    return lax.dot_general(a, b, (((1,), (0,)), ((), ())), preferred_element_type=F32)


def dot_nt(a, b):
    return lax.dot_general(a, b, (((1,), (1,)), ((), ())), preferred_element_type=F32)


def gelu(v):
    return 0.5 * v * (1.0 + jnp.tanh(GELU_A * (v + GELU_B * v * v * v)))


def gelu_slope(v):
    t = jnp.tanh(GELU_A * (v + GELU_B * v * v * v))
    inner = GELU_A * (1.0 + 3.0 * GELU_B * v * v)
    return 0.5 * (1.0 + t) + 0.5 * v * (1.0 - t * t) * inner


def tile_at(n, size):
    return pl.ds(pl.multiple_of(n * size, size), size)


def kernel(
    total_rows,
    feat,
    w_in,
    w_out,
    labels_hbm,
    pairs,
    fg_out,
    ig_out,
    og_out,
    loss_out,
    fx,
    wi,
    wo,
    pre,
    hid,
    emb,
    uni,
    labels,
    slope,
    ups,
    back,
    quarter,
    turned,
    gs,
    r0,
    s0,
    r1,
    s1,
    r2,
    s2,
    r3,
    s3,
    ag,
    lk,
    ly,
    lx,
    lz,
    lz2,
    ssem,
    rsem,
    lsem,
):
    pair = lax.axis_index("pair")
    shard = lax.axis_index("shard")
    x, zh = pair // 2, pair % 2
    zl, y, k = shard // 8, (shard // 2) % 4, shard % 2
    z = zh * 4 + zl
    far = 1 - zh

    def device(dx=0, dy=0, dz=0, dk=0):
        zz = (z + dz + 8) % 8
        return (
            ((x + dx + 4) % 4) * 2 + zz // 4,
            (zz % 4) * 8 + ((y + dy + 4) % 4) * 2 + (k + dk) % 2,
        )

    started = []

    def send(src, dst, **offset):
        i = len(started)
        copy = pltpu.make_async_remote_copy(
            src_ref=src,
            dst_ref=dst,
            send_sem=ssem.at[i],
            recv_sem=rsem.at[i],
            device_id=device(**offset),
            device_id_type=MESH,
        )
        copy.start()
        started.append(copy)
        return copy

    def arrive(copies):
        for copy in copies:
            copy.wait_recv()

    inputs = [
        pltpu.make_async_copy(w_in, wi.at[zl, y, k], lsem.at[0]),
        pltpu.make_async_copy(w_out, wo.at[zl, y, k], lsem.at[1]),
        pltpu.make_async_copy(feat, fx.at[zh, x], lsem.at[2]),
        pltpu.make_async_copy(labels_hbm, labels, lsem.at[3]),
    ]
    for copy in inputs:
        copy.start()

    barrier = pltpu.get_barrier_semaphore()
    partners = (
        [dict(dx=d) for d in (1, -1, 2)]
        + [dict(dy=d) for d in (1, -1, 2)]
        + [dict(dz=d) for d in (1, -1, 2, -2, 4)]
        + [dict(dk=1)]
    )
    for offset in partners:
        pl.semaphore_signal(barrier, inc=1, device_id=device(**offset), device_id_type=MESH)
    lz[...] = jnp.zeros_like(lz)
    pl.semaphore_wait(barrier, len(partners))

    sources, held = (w_in, w_out), (wi, wo)
    zl_of = (zl, (zl + 3) % 4, (zl + 1) % 4, (zl + 2) % 4)
    from_z, from_y, from_y2, from_core = {}, {}, {}, {}
    from_far, from_x, from_x_far = {}, [], {}

    def along_z(t):
        src, dst = sources[t], held[t].at[zl, y, k]
        from_z[t, 1] = [send(src, dst, dz=1)]
        from_z[t, 2] = [send(src, dst, dz=-1)]
        from_z[t, 3] = [
            send(src.at[h], dst.at[h], dz=d) for h, d in ((pl.ds(0, 16), 2), (pl.ds(16, 16), -2))
        ]

    def along_y(t, j):
        dst = held[t].at[zl_of[j], y, k]
        if j:
            arrive(from_z[t, j])
        src = dst if j else sources[t]
        from_y[t, j] = [send(src, dst, dy=1), send(src, dst, dy=-1)]

    def pass_on(t, j):
        from_below, from_above = from_y[t, j]
        copies = []
        for copy, d, h in ((from_below, 1, 0), (from_above, -1, 16)):
            copy.wait_recv()
            block = held[t].at[zl_of[j], (y - d + 4) % 4, k, pl.ds(h, 16)]
            copies.append(send(block, block, dy=d))
        from_y2[t, j] = copies

    def to_core(t, j):
        arrive(from_y2[t, j])
        half = held[t].at[zl_of[j], :, k]
        from_core[t, j] = send(half, half, dk=1)

    def piece(i):
        return pl.ds(i * 32, 32)

    def to_far(i):
        from_far[i] = send(feat.at[piece(i)], fx.at[zh, x, piece(i)], dz=4)

    def far_along_x(i):
        from_far[i].wait_recv()
        block = fx.at[far, x, piece(i)]
        from_x_far[i] = [send(block, block, dx=d) for d in (1, -1, 2)]

    def turn(t, src):
        def step(b, carry):
            for n in range(8):
                block = src[zh, b, :, n * 128 : n * 128 + 128].T
                turned[t, n * 4 : n * 4 + 4, :, tile_at(b, 128)] = block.reshape(4, 32, 128)
            return carry

        lax.fori_loop(0, 4, step, 0)

    def hidden_near():
        def step(n, carry):
            cols = tile_at(n, 256)
            acc = dot_nn(fx[zh].reshape(512, WIDTH), wi[:, :, :, :, cols].reshape(WIDTH, 256))
            pre[:, cols] = acc
            hid[zh, :, :, cols] = gelu(acc).astype(BF16).reshape(4, 128, 256)
            return carry

        lax.fori_loop(0, 4, step, 0)

    def hidden_far(h):
        rows = pl.ds(h * 64, 64)

        def step(n, carry):
            cols = tile_at(n, 256)
            acc = dot_nn(
                fx[far, :, rows, :].reshape(256, WIDTH), wi[:, :, :, :, cols].reshape(WIDTH, 256)
            )
            hid[far, :, rows, cols] = gelu(acc).astype(BF16).reshape(4, 64, 256)
            return carry

        lax.fori_loop(0, 4, step, 0)

    def embed_of(group):
        def step(n, carry):
            cols = tile_at(n, 256)
            emb[group, :, cols] = dot_nn(
                hid[group].reshape(512, WIDTH), wo[:, :, :, :, cols].reshape(WIDTH, 256)
            )
            return carry

        lax.fori_loop(0, 4, step, 0)

        def norm(n, carry):
            rows = tile_at(n, 64)
            v = emb[group, rows, :]
            mean_square = jnp.mean(v * v, axis=-1, keepdims=True) + EPSILON
            uni[group, rows, :] = (v * (lax.rsqrt(mean_square) / math.sqrt(WIDTH))).astype(BF16)
            return carry

        lax.fori_loop(0, 8, norm, 0)

    along_z(0)
    along_y(0, 0)
    from_x = [send(feat, fx.at[zh, x], dx=d) for d in (1, -1, 2)]
    to_far(0)
    to_far(1)
    along_y(1, 0)
    for copy in inputs:
        copy.wait()
    pass_on(0, 0)
    along_y(0, 1)
    along_y(0, 2)
    along_y(0, 3)
    along_z(1)
    to_far(2)
    to_far(3)
    pass_on(1, 0)
    pass_on(0, 1)
    far_along_x(0)
    pass_on(0, 2)
    pass_on(0, 3)
    to_core(0, 0)
    to_core(0, 1)
    far_along_x(1)
    to_core(0, 2)
    to_core(0, 3)
    along_y(1, 1)
    along_y(1, 2)
    along_y(1, 3)
    to_core(1, 0)
    arrive(from_x)
    turn(0, fx)
    arrive([from_core[0, j] for j in range(4)])
    hidden_near()
    pass_on(1, 1)
    pass_on(1, 2)
    pass_on(1, 3)
    far_along_x(2)
    turn(1, hid)
    arrive(from_x_far[0] + from_x_far[1])
    hidden_far(0)
    far_along_x(3)
    to_core(1, 1)
    to_core(1, 2)
    to_core(1, 3)
    arrive([from_core[1, j] for j in range(4)])
    embed_of(zh)
    arrive(from_x_far[2] + from_x_far[3])
    hidden_far(1)
    embed_of(far)

    own = tile_at(x, 128)
    codes = [pairs[i, 0] * 8 + pairs[i, 1] for i in range(16)]
    own_labels = jnp.broadcast_to(labels[pl.ds(pair, 1), :].astype(F32), (128, 128)).T
    loss_sum = jnp.zeros((128, 128), F32)
    for g in range(2):
        scores = dot_nt(uni[zh, own, :], uni[g])
        for i in range(4):
            q = i * 2 + g
            target = jnp.minimum(pair, q) * 8 + jnp.maximum(pair, q)
            listed = functools.reduce(
                lambda a, b: a + b, [jnp.where(c == target, 1.0, 0.0) for c in codes]
            )
            twice = jnp.where(pair == q, 2.0, 1.0)
            counted = jnp.where(pair <= q, 1.0, 0.0)
            logits = SIM_SCALE * scores[:, i * 128 : i * 128 + 128] + SIM_OFFSET
            same = own_labels == labels[q : q + 1, :].astype(F32)
            sign = jnp.where(same, 1.0, -1.0)
            margin = sign * logits
            small = jnp.exp(-jnp.abs(margin))
            loss_sum += (listed * counted) * (jnp.maximum(-margin, 0.0) + jnp.log1p(small))
            share = jnp.where(margin >= 0.0, small, 1.0) / (1.0 + small)
            slope[:, g * 512 + i * 128 : g * 512 + i * 128 + 128] = (
                (-LOSS_SCALE * SIM_SCALE * sign * share).astype(BF16).astype(F32)
                * (listed * twice)
            ).astype(BF16)
    loss_total = jnp.broadcast_to(
        jnp.sum(jnp.sum(loss_sum, axis=0, keepdims=True), axis=1, keepdims=True), (8, 128)
    )
    lk[k] = loss_total
    loss_core = send(lk.at[k], lk.at[k], dk=1)

    def upstream(n, carry):
        cols = tile_at(n, 256)
        ups[:, cols] = dot_nn(slope[...], uni[:, :, cols].reshape(WIDTH, 256))
        return carry

    lax.fori_loop(0, 4, upstream, 0)

    def embed_back(n, carry):
        rows = tile_at(n, 32)
        v = emb[zh, pl.ds(pl.multiple_of(x * 128 + n * 32, 32), 32), :]
        up = ups[rows, :]
        mean_square = jnp.mean(v * v, axis=-1, keepdims=True) + EPSILON
        inverse = lax.rsqrt(mean_square) / math.sqrt(WIDTH)
        projected = jnp.sum(up * v, axis=-1, keepdims=True)
        grad = inverse * up - v * (inverse / (WIDTH * mean_square)) * projected
        back[1, rows, :] = grad.astype(BF16)
        return carry

    lax.fori_loop(0, 4, embed_back, 0)

    def quarters(t):
        copies = [
            send(back.at[t, :, tile_at((x + d + 4) % 4, 256)], quarter.at[t, x], dx=d)
            for d in (1, -1, 2)
        ]
        quarter[t, x] = back[t, :, tile_at(x, 256)]
        return copies

    out_q = quarters(1)
    loss_core.wait_recv()
    ly[y] = lk[0] + lk[1]
    loss_y = [send(ly.at[y], ly.at[y], dy=d) for d in (1, -1, 2)]

    def hidden_back(n, carry):
        cols = tile_at(n, 256)
        hidden_grad = dot_nt(back[1], wo[n].reshape(256, WIDTH))
        back[0, :, cols] = (hidden_grad * gelu_slope(pre[own, cols])).astype(BF16)
        return carry

    lax.fori_loop(0, 4, hidden_back, 0)
    in_q = quarters(0)
    arrive(loss_y)
    lx[x] = (ly[0] + ly[1]) + (ly[2] + ly[3])
    loss_x = [send(lx.at[x], lx.at[x], dx=d) for d in (1, -1, 2)]

    def weight_grad(t, copies):
        arrive(copies)

        def step(n, carry):
            grad = dot_nn(
                turned[t, pl.ds(pl.multiple_of(n * 8, 8), 8)].reshape(256, 512),
                quarter[t].reshape(512, 256),
            )
            gs[t, n] = grad.astype(BF16).reshape(4, 2, 32, 256)
            return carry

        lax.fori_loop(0, 4, step, 0)
        return send(gs.at[t, :, :, 1 - k], r0.at[t], dk=1)

    out_0 = weight_grad(1, out_q)
    in_0 = weight_grad(0, in_q)

    def add_core(t, copy):
        copy.wait_recv()
        for i in range(4):
            s0[t, i] = (gs[t, i, :, k].astype(F32) + r0[t, i].astype(F32)).astype(BF16)

    def add(mine, received):
        total = mine.astype(F32)
        for j in range(3):
            total += received[j].astype(F32)
        return total.astype(BF16)

    def sum_y(src, dst):
        return [send(src((y + d + 4) % 4), dst.at[i], dy=d) for i, d in enumerate((1, -1, 2))]

    def sum_z(src, dst, half):
        across = src((zl + 2) % 4)
        low, high = pl.ds(0, half), pl.ds(half, half)
        return [
            send(src((zl + 1) % 4), dst.at[0], dz=1),
            send(src((zl + 3) % 4), dst.at[1], dz=-1),
            send(across.at[low], dst.at[2, low], dz=2),
            send(across.at[high], dst.at[2, high], dz=-2),
        ]

    add_core(1, out_0)
    out_1 = sum_y(lambda i: s0.at[1, :, i], r1.at[1])
    add_core(0, in_0)
    in_1 = sum_z(lambda i: s0.at[0, i], r1.at[0], 2)
    arrive(loss_x)
    lz[z] = (lx[0] + lx[1]) + (lx[2] + lx[3])
    loss_z = [send(lz.at[z], lz.at[z], dz=d) for d in (1, -1, 2, -2)]

    def feature_back(n, carry):
        cols = tile_at(n, 256)
        fg_out[:, cols] = dot_nt(back[0], wi[n].reshape(256, WIDTH)).astype(BF16)
        return carry

    lax.fori_loop(0, 4, feature_back, 0)

    arrive(out_1)
    s1[1] = add(s0[1, :, y], r1[1])
    out_2 = sum_z(lambda i: s1.at[1, i], r2.at[1], 16)
    arrive(in_1)
    s1[0] = add(s0[0, zl], r1[0])
    in_2 = sum_y(lambda i: s1.at[0, i], r2.at[0])
    arrive(loss_z)
    loss_far = send(lz, lz2, dz=4)

    def sum_far(t, mine, copies):
        arrive(copies)
        s2[t] = add(s1[t, mine], r2[t])
        return send(s2.at[t], r3.at[t], dz=4)

    out_3 = sum_far(1, zl, out_2)
    in_3 = sum_far(0, y, in_2)

    def spread(t, copy):
        copy.wait_recv()
        s3[t] = (s2[t].astype(F32) + r3[t].astype(F32)).astype(BF16)
        cols = tile_at(x, 256)
        copies = [send(s3.at[t], ag.at[t, :, cols], dx=d) for d in (1, -1, 2)]
        ag[t, :, cols] = s3[t]
        return copies

    out_4 = spread(1, out_3)
    in_4 = spread(0, in_3)

    loss_far.wait_recv()
    loss = jnp.zeros((8, 128), F32)
    for i in range(8):
        away = (i - z + 8) % 8
        near = jnp.where(away <= 2, 1, jnp.where(away >= 6, 1, 0))
        loss += jnp.where(near == 1, lz[i], lz2[i])
    loss_out[...] = loss / total_rows

    factor = 1.0 / math.sqrt(total_rows)
    arrive(out_4)
    og_out[...] = ag[1].astype(F32) * factor
    arrive(in_4)
    ig_out[...] = ag[0].astype(F32) * factor
    for copy in started:
        copy.wait_send()


def per_device(features, w_in, w_out, labels, pair_list):
    total_rows = lax.axis_size("pair") * lax.axis_size("shard") * features.shape[1]
    vmem = pl.BlockSpec(memory_space=pltpu.VMEM)
    smem = pl.BlockSpec(memory_space=pltpu.SMEM)
    hbm = pl.BlockSpec(memory_space=pltpu.HBM)
    w = WIDTH
    fg, ig, og, loss = pl.pallas_call(
        functools.partial(kernel, total_rows),
        name="contrastive_step",
        out_shape=(
            jax.ShapeDtypeStruct((128, w), BF16),
            jax.ShapeDtypeStruct((32, w), F32),
            jax.ShapeDtypeStruct((32, w), F32),
            jax.ShapeDtypeStruct((8, 128), F32),
        ),
        in_specs=[hbm, hbm, hbm, hbm, smem],
        out_specs=(vmem, vmem, vmem, vmem),
        scratch_shapes=[
            pltpu.VMEM((2, 4, 128, w), BF16),
            pltpu.VMEM((4, 4, 2, 32, w), BF16),
            pltpu.VMEM((4, 4, 2, 32, w), BF16),
            pltpu.VMEM((512, w), F32),
            pltpu.VMEM((2, 4, 128, w), BF16),
            pltpu.VMEM((2, 512, w), F32),
            pltpu.VMEM((2, 512, w), BF16),
            pltpu.VMEM((8, 128), jnp.int32),
            pltpu.VMEM((128, w), BF16),
            pltpu.VMEM((128, w), F32),
            pltpu.VMEM((2, 128, w), BF16),
            pltpu.VMEM((2, 4, 128, 256), BF16),
            pltpu.VMEM((2, 32, 32, 512), BF16),
            pltpu.VMEM((2, 4, 4, 2, 32, 256), BF16),
            pltpu.VMEM((2, 4, 4, 32, 256), BF16),
            pltpu.VMEM((2, 4, 4, 32, 256), BF16),
            pltpu.VMEM((2, 3, 4, 32, 256), BF16),
            pltpu.VMEM((2, 4, 32, 256), BF16),
            pltpu.VMEM((2, 3, 32, 256), BF16),
            pltpu.VMEM((2, 32, 256), BF16),
            pltpu.VMEM((2, 32, 256), BF16),
            pltpu.VMEM((2, 32, 256), BF16),
            pltpu.VMEM((2, 32, w), BF16),
            pltpu.VMEM((2, 8, 128), F32),
            pltpu.VMEM((4, 8, 128), F32),
            pltpu.VMEM((4, 8, 128), F32),
            pltpu.VMEM((8, 8, 128), F32),
            pltpu.VMEM((8, 8, 128), F32),
            pltpu.SemaphoreType.DMA((COPIES,)),
            pltpu.SemaphoreType.DMA((COPIES,)),
            pltpu.SemaphoreType.DMA((4,)),
        ],
        compiler_params=pltpu.CompilerParams(
            collective_id=0, has_side_effects=True, vmem_limit_bytes=48 * 2**20
        ),
    )(features[0], w_in, w_out, labels, pair_list)
    return fg[None], ig, og, loss[0, 0]


def solution(mesh):
    in_specs = (
        P("pair", "shard", None),
        P("shard", None),
        P("shard", None),
        P(None, "shard"),
        P("shard", None),
    )
    out_specs = (P("pair", "shard", None), P("shard", None), P("shard", None), P())
    return jax.shard_map(
        per_device, mesh=mesh, in_specs=in_specs, out_specs=out_specs, check_vma=False
    )
```

time: 99.5 us -> 83.1 us (0.84); the launches traced: 97.7 us -> 82.9 us
  Pallas kernels: 90.5 us -> 75.7 us
    pallas_call x1, Pallas kernels: 90.5 us -> 75.7 us  [per_device(): pl.pallas_call(functools.partial(kernel, total_rows), name='contrastive_s...]
where the time goes in v2:
time: 83.1 us; the launch traced here: 82.9 us
  Pallas kernels  75.7 us (91%)
  local copies, waits for them, and re-layouts  6.51 us (8%)
    pallas_call x1, Pallas kernels, per_device(): pl.pallas_call(functools.partial(kernel, total_rows), name='contrastive_s...  75.7 us
    unnamed x14, local copies, waits for them, and re-layouts  6 us

profile of v2, /device:TPU:1, one launch (start us, length us, event | category | flops | bytes accessed | tf_op | source)
XLA Modules:
  0.0 82.9 jit_solution(16457765762251323878)
XLA Ops:
  0.6 0.0 copy-start.4
  0.6 0.7 copy-done.4
  1.3 0.0 copy-start.3
  1.3 0.1 copy.9.pairs
  1.4 0.6 copy-done.3
  2.0 0.0 copy-start
  2.0 0.9 %copy-done = bf16[1,128,1024]{2,1,0:T(8,128)(2,1)S(1)} copy-done((bf16[1,128,1024]{2,1,0:T(8,128)(2,1)S(1)}, bf16[1,128,1024]{2,1,0:T(8,128)(2,1)}, u32[]{:S(2)}) %copy-start) | copy-done | bytes 262168
  2.9 0.0 copy-start.1
  3.0 0.8 %copy-done.1 = bf16[32,1024]{1,0:T(8,128)(2,1)S(1)} copy-done((bf16[32,1024]{1,0:T(8,128)(2,1)S(1)}, bf16[32,1024]{1,0:T(8,128)(2,1)}, u32[]{:S(2)}) %copy-start.1) | copy-done | bytes 65560
  3.8 0.0 copy-start.2
  3.8 0.8 %copy-done.2 = bf16[32,1024]{1,0:T(8,128)(2,1)S(1)} copy-done((bf16[32,1024]{1,0:T(8,128)(2,1)S(1)}, bf16[32,1024]{1,0:T(8,128)(2,1)}, u32[]{:S(2)}) %copy-start.2) | copy-done | bytes 65560
  4.6 75.7 %contrastive_step.1 = (bf16[128,1024]{1,0:T(8,128)(2,1)S(1)}, f32[32,1024]{1,0:T(8,128)S(1)}, f32[32,1024]{1,0:T(8,128)S(1)}, f32[8,128]{1,0:T(8,128)S(1)}) custom-call(bf16[128,1024]{1,0:T(8,128)(2,1)S(1)} %bitcast.3, bf16[32,1024]{1,0:T(8,128)(2,1)S(1)} %copy-done.1, bf16[32,1024]{1,0:T(8,128)(2,1)S(1)} %copy-done.2, s32[8,128]{1,0:T(8,128)S(1)} %copy-done.3, ...), custom_call_target="tpu_custom_call" | custom-call | tf_op jit(solution)/shard_map/contrastive_step/pallas_call | solution.py:474
  80.3 0.5 slice.3
  80.9 0.7 copy.13
  81.6 0.7 copy.14
  82.2 0.7 copy.15
Async XLA Ops:
  0.6 0.7 copy-start.4
  1.3 0.7 copy-start.3
  2.0 0.9 %copy-start = (bf16[1,128,1024]{2,1,0:T(8,128)(2,1)S(1)}, bf16[1,128,1024]{2,1,0:T(8,128)(2,1)}, u32[]{:S(2)}) copy-start(bf16[1,128,1024]{2,1,0:T(8,128)(2,1)} %param.5) | copy-start | bytes 786436
  2.9 0.8 %copy-start.1 = (bf16[32,1024]{1,0:T(8,128)(2,1)S(1)}, bf16[32,1024]{1,0:T(8,128)(2,1)}, u32[]{:S(2)}) copy-start(bf16[32,1024]{1,0:T(8,128)(2,1)} %w_in.1) | copy-start | bytes 196612
  3.8 0.8 %copy-start.2 = (bf16[32,1024]{1,0:T(8,128)(2,1)S(1)}, bf16[32,1024]{1,0:T(8,128)(2,1)}, u32[]{:S(2)}) copy-start(bf16[32,1024]{1,0:T(8,128)(2,1)} %w_out.1) | copy-start | bytes 196612

commit v3 on v2

v3 whole, which is shorter than its diff:
```python
import functools
import math

import jax
import jax.numpy as jnp
from jax import lax
from jax.experimental import pallas as pl
from jax.experimental.pallas import tpu as pltpu
from jax.sharding import PartitionSpec as P

MESH = pl.DeviceIdType.MESH
BF16 = jnp.bfloat16
F32 = jnp.float32

EPSILON = 1e-06
SIM_SCALE = 10.0
SIM_OFFSET = -5.0
LOSS_SCALE = 256.0
WIDTH = 1024
GELU_A = math.sqrt(2.0 / math.pi)
GELU_B = 0.044715
COPIES = 160
ACROSS = (1, -1, 2, -2, 3, -3, 4)


def dot_nn(a, b):
    return lax.dot_general(a, b, (((1,), (0,)), ((), ())), preferred_element_type=F32)


def dot_nt(a, b):
    return lax.dot_general(a, b, (((1,), (1,)), ((), ())), preferred_element_type=F32)


def gelu(v):
    return 0.5 * v * (1.0 + jnp.tanh(GELU_A * (v + GELU_B * v * v * v)))


def gelu_slope(v):
    t = jnp.tanh(GELU_A * (v + GELU_B * v * v * v))
    inner = GELU_A * (1.0 + 3.0 * GELU_B * v * v)
    return 0.5 * (1.0 + t) + 0.5 * v * (1.0 - t * t) * inner


def tile_at(n, size):
    return pl.ds(pl.multiple_of(n * size, size), size)


def kernel(
    total_rows,
    feat,
    w_in,
    w_out,
    labels_hbm,
    pairs,
    fg_out,
    ig_out,
    og_out,
    loss_out,
    fx,
    wi,
    wo,
    pre,
    hid,
    emb,
    uni,
    labels,
    ids,
    sign,
    slope,
    ups,
    back,
    quarter,
    turned,
    gs,
    r0,
    s0,
    r1,
    s1,
    r2,
    s3,
    ag,
    lk,
    ly,
    lx,
    lz,
    ssem,
    rsem,
    lsem,
):
    pair = lax.axis_index("pair")
    shard = lax.axis_index("shard")
    x, zh = pair // 2, pair % 2
    zl, y, k = shard // 8, (shard // 2) % 4, shard % 2
    z = zh * 4 + zl
    far = 1 - zh

    def device(dx=0, dy=0, dz=0, dk=0):
        zz = (z + dz + 8) % 8
        return (
            ((x + dx + 4) % 4) * 2 + zz // 4,
            (zz % 4) * 8 + ((y + dy + 4) % 4) * 2 + (k + dk) % 2,
        )

    started = []

    def send(src, dst, **offset):
        i = len(started)
        copy = pltpu.make_async_remote_copy(
            src_ref=src,
            dst_ref=dst,
            send_sem=ssem.at[i],
            recv_sem=rsem.at[i],
            device_id=device(**offset),
            device_id_type=MESH,
        )
        copy.start()
        started.append(copy)
        return copy

    def arrive(copies):
        for copy in copies:
            copy.wait_recv()

    inputs = [
        pltpu.make_async_copy(w_in, wi.at[zl, y, k], lsem.at[0]),
        pltpu.make_async_copy(w_out, wo.at[zl, y, k], lsem.at[1]),
        pltpu.make_async_copy(feat, fx.at[zh, x], lsem.at[2]),
        pltpu.make_async_copy(labels_hbm, labels, lsem.at[3]),
    ]
    for copy in inputs:
        copy.start()

    barrier = pltpu.get_barrier_semaphore()
    partners = (
        [dict(dx=d) for d in (1, -1, 2)]
        + [dict(dy=d) for d in (1, -1, 2)]
        + [dict(dz=d) for d in ACROSS]
        + [dict(dk=1)]
    )
    for offset in partners:
        pl.semaphore_signal(barrier, inc=1, device_id=device(**offset), device_id_type=MESH)
    pl.semaphore_wait(barrier, len(partners))

    sources, held = (w_in, w_out), (wi, wo)
    zl_of = (zl, (zl + 3) % 4, (zl + 1) % 4, (zl + 2) % 4)
    from_z, from_y, from_y2, from_core = {}, {}, {}, {}
    from_far, from_x, from_x_far = {}, [], {}

    def along_z(t):
        src, dst = sources[t], held[t].at[zl, y, k]
        from_z[t, 1] = [send(src, dst, dz=1)]
        from_z[t, 2] = [send(src, dst, dz=-1)]
        from_z[t, 3] = [
            send(src.at[h], dst.at[h], dz=d) for h, d in ((pl.ds(0, 16), 2), (pl.ds(16, 16), -2))
        ]

    def along_y(t, j):
        dst = held[t].at[zl_of[j], y, k]
        if j:
            arrive(from_z[t, j])
        src = dst if j else sources[t]
        from_y[t, j] = [send(src, dst, dy=1), send(src, dst, dy=-1)]

    def pass_on(t, j):
        from_below, from_above = from_y[t, j]
        copies = []
        for copy, d, h in ((from_below, 1, 0), (from_above, -1, 16)):
            copy.wait_recv()
            block = held[t].at[zl_of[j], (y - d + 4) % 4, k, pl.ds(h, 16)]
            copies.append(send(block, block, dy=d))
        from_y2[t, j] = copies

    def to_core(t, j):
        arrive(from_y2[t, j])
        half = held[t].at[zl_of[j], :, k]
        from_core[t, j] = send(half, half, dk=1)

    def pass_x():
        copies = []
        for copy, d, h in ((from_x[0], 1, 0), (from_x[1], -1, 64)):
            copy.wait_recv()
            block = fx.at[zh, (x - d + 4) % 4, pl.ds(h, 64)]
            copies.append(send(block, block, dx=d))
        return copies

    def piece(i):
        return pl.ds(i * 32, 32)

    def to_far(i):
        from_far[i] = send(feat.at[piece(i)], fx.at[zh, x, piece(i)], dz=4)

    def far_along_x(i):
        from_far[i].wait_recv()
        block = fx.at[far, x, piece(i)]
        from_x_far[i] = [send(block, block, dx=d) for d in (1, -1, 2)]

    def turn(t, read):
        def step(b, carry):
            for n in range(8):
                block = read(b, slice(n * 128, n * 128 + 128)).T
                turned[t, n * 4 : n * 4 + 4, :, tile_at(b, 128)] = block.reshape(4, 32, 128)
            return carry

        lax.fori_loop(0, 4, step, 0)

    def hidden_near():
        acc = dot_nn(fx[zh].reshape(512, WIDTH), wi[...].reshape(WIDTH, WIDTH))
        pre[...] = acc
        hid[0:512, :] = gelu(acc).astype(BF16)

    def hidden_far(h):
        rows = fx[far, :, h * 64 : h * 64 + 64, :].reshape(256, WIDTH)
        acc = dot_nn(rows, wi[...].reshape(WIDTH, WIDTH))
        hid[512 + h * 256 : 768 + h * 256, :] = gelu(acc).astype(BF16)

    def embed(start, size):
        for i in range(start, start + size, 256):
            v = dot_nn(hid[i : i + 256, :], wo[...].reshape(WIDTH, WIDTH))
            emb[i : i + 256, :] = v
        for i in range(start, start + size, 256):
            v = emb[i : i + 256, :]
            mean_square = jnp.mean(v * v, axis=-1, keepdims=True) + EPSILON
            uni[i : i + 256, :] = (v * (lax.rsqrt(mean_square) / math.sqrt(WIDTH))).astype(BF16)

    own = tile_at(x, 128)

    def score(start, size):
        scores = dot_nt(uni[own, :], uni[start : start + size, :])
        total = jnp.zeros((128, 128), F32)
        for i in range(size // 128):
            b = start // 128 + i
            cols = slice(b * 128, b * 128 + 128)
            same_sign = sign[:, cols]
            margin = same_sign * (
                SIM_SCALE * scores[:, i * 128 : i * 128 + 128] + SIM_OFFSET
            )
            small = jnp.exp(-jnp.abs(margin))
            total += loss_rows[b] * (jnp.maximum(-margin, 0.0) + jnp.log1p(small))
            share = jnp.where(margin >= 0.0, small, 1.0) / (1.0 + small)
            slope[:, cols] = (slope_rows[b] * (same_sign * share)).astype(BF16)
        return total

    def upstream(start, size):
        part = dot_nn(slope[:, start : start + size], uni[start : start + size, :])
        ups[...] = part if start == 0 else ups[...] + part

    along_z(0)
    along_y(0, 0)
    from_x = [send(feat, fx.at[zh, x], dx=d) for d in (1, -1)]
    to_far(0)
    along_y(1, 0)

    codes = [pairs[i, 0] * 8 + pairs[i, 1] for i in range(16)]

    def pair_weights(q):
        target = jnp.minimum(pair, q) * 8 + jnp.maximum(pair, q)
        listed = functools.reduce(
            lambda a, b: a + b, [jnp.where(c == target, 1.0, 0.0) for c in codes]
        )
        scale = -LOSS_SCALE * SIM_SCALE * jnp.where(pair == q, 2.0, 1.0)
        return listed * scale, listed * jnp.where(pair <= q, 1.0, 0.0)

    for copy in inputs:
        copy.wait()
    ids[0] = labels[...].astype(F32)
    ids[1] = pltpu.roll(ids[0], 64, 1)
    own_ids = jnp.broadcast_to(ids[0, pl.ds(pair, 1), :], (128, 128)).T
    lane = lax.broadcasted_iota(jnp.int32, (1, 128), 1)
    slope_rows, loss_rows = [], []

    def same_label(b, row):
        sign[:, b * 128 : b * 128 + 128] = jnp.where(own_ids == row, 1.0, -1.0)

    for b in range(4):
        q = b * 2 + zh
        on_slope, on_loss = pair_weights(q)
        slope_rows.append(jnp.full((1, 128), on_slope, F32))
        loss_rows.append(jnp.full((1, 128), on_loss, F32))
        same_label(b, ids[0, pl.ds(q, 1), :])
    far_weights = [pair_weights(b * 2 + far) for b in range(4)]
    for h in range(2):
        for c in range(2):
            low, high = far_weights[2 * c], far_weights[2 * c + 1]
            slope_rows.append(jnp.where(lane < 64, low[0], high[0]))
            loss_rows.append(jnp.where(lane < 64, low[1], high[1]))
            row = jnp.where(
                lane < 64,
                ids[h, pl.ds(4 * c + far, 1), :],
                ids[1 - h, pl.ds(4 * c + 2 + far, 1), :],
            )
            same_label(4 + 2 * h + c, row)
    pass_on(0, 0)
    along_y(0, 1)
    along_y(0, 2)
    to_far(1)
    along_y(0, 3)
    along_z(1)
    pass_on(1, 0)
    to_far(2)
    from_x2 = pass_x()
    pass_on(0, 1)
    to_far(3)
    pass_on(0, 2)
    far_along_x(0)
    pass_on(0, 3)
    along_y(1, 1)
    along_y(1, 2)
    along_y(1, 3)
    far_along_x(1)
    for j in range(4):
        to_core(0, j)
    pass_on(1, 1)
    arrive(from_x2)
    turn(0, lambda b, cols: fx[zh, b, :, cols])
    pass_on(1, 2)
    arrive([from_core[0, j] for j in range(4)])
    far_along_x(2)
    hidden_near()
    pass_on(1, 3)
    far_along_x(3)
    for j in range(4):
        to_core(1, j)
    turn(1, lambda b, cols: hid[tile_at(b, 128), cols])
    arrive(from_x_far[0] + from_x_far[1])
    hidden_far(0)
    arrive([from_core[1, j] for j in range(4)])
    embed(0, 768)
    loss_sum = score(0, 512)
    loss_sum += score(512, 256)
    upstream(0, 768)
    arrive(from_x_far[2] + from_x_far[3])
    hidden_far(1)
    embed(768, 256)
    loss_sum += score(768, 256)
    upstream(768, 256)
    loss_total = jnp.broadcast_to(
        jnp.sum(jnp.sum(loss_sum, axis=0, keepdims=True), axis=1, keepdims=True), (8, 128)
    )
    lk[k] = loss_total
    loss_core = send(lk.at[k], lk.at[k], dk=1)

    v = emb[own, :]
    up = ups[...]
    mean_square = jnp.mean(v * v, axis=-1, keepdims=True) + EPSILON
    inverse = lax.rsqrt(mean_square) / math.sqrt(WIDTH)
    projected = jnp.sum(up * v, axis=-1, keepdims=True)
    grad = inverse * up - v * (inverse / (WIDTH * mean_square)) * projected
    back[1] = grad.astype(BF16)

    def quarters(t):
        copies = [
            send(back.at[t, :, tile_at((x + d + 4) % 4, 256)], quarter.at[t, x], dx=d)
            for d in (1, -1, 2)
        ]
        quarter[t, x] = back[t, :, tile_at(x, 256)]
        return copies

    out_q = quarters(1)
    loss_core.wait_recv()
    ly[y] = lk[0] + lk[1]
    loss_y = [send(ly.at[y], ly.at[y], dy=d) for d in (1, -1, 2)]

    hidden_grad = dot_nt(back[1], wo[...].reshape(WIDTH, WIDTH))
    back[0] = (hidden_grad * gelu_slope(pre[own, :])).astype(BF16)
    in_q = quarters(0)
    arrive(loss_y)
    lx[x] = (ly[0] + ly[1]) + (ly[2] + ly[3])
    loss_x = [send(lx.at[x], lx.at[x], dx=d) for d in (1, -1, 2)]

    def weight_grad(t, copies):
        arrive(copies)

        grad = dot_nn(turned[t].reshape(WIDTH, 512), quarter[t].reshape(512, 256))
        gs[t] = grad.astype(BF16).reshape(4, 4, 2, 32, 256)
        return send(gs.at[t, :, :, 1 - k], r0.at[t], dk=1)

    out_0 = weight_grad(1, out_q)
    in_0 = weight_grad(0, in_q)

    def add_core(t, copy):
        copy.wait_recv()
        for i in range(4):
            s0[t, i] = (gs[t, i, :, k].astype(F32) + r0[t, i].astype(F32)).astype(BF16)

    def add(mine, received):
        total = mine.astype(F32)
        for j in range(3):
            total += received[j].astype(F32)
        return total.astype(BF16)

    def sum_y(src, dst):
        return [send(src((y + d + 4) % 4), dst.at[i], dy=d) for i, d in enumerate((1, -1, 2))]

    def sum_z(t):
        copies = [send(s1.at[t, (zl + d + 4) % 4], r2.at[t, z], dz=d) for d in ACROSS]
        r2[t, z] = s1[t, zl]
        return copies

    add_core(1, out_0)
    out_1 = sum_y(lambda i: s0.at[1, :, i], r1.at[1])
    add_core(0, in_0)
    in_1 = sum_y(lambda i: s0.at[0, :, i], r1.at[0])
    arrive(loss_x)
    lz[z] = (lx[0] + lx[1]) + (lx[2] + lx[3])
    loss_z = [send(lz.at[z], lz.at[z], dz=d) for d in ACROSS]

    fg_out[...] = dot_nt(back[0], wi[...].reshape(WIDTH, WIDTH)).astype(BF16)

    arrive(out_1)
    s1[1] = add(s0[1, :, y], r1[1])
    out_2 = sum_z(1)
    arrive(in_1)
    s1[0] = add(s0[0, :, y], r1[0])
    in_2 = sum_z(0)

    def spread(t, copies):
        arrive(copies)
        total = r2[t, 0].astype(F32)
        for i in range(1, 8):
            total += r2[t, i].astype(F32)
        s3[t] = total.astype(BF16)
        cols = tile_at(x, 256)
        copies = [send(s3.at[t], ag.at[t, :, cols], dx=d) for d in (1, -1, 2)]
        ag[t, :, cols] = s3[t]
        return copies

    out_4 = spread(1, out_2)
    in_4 = spread(0, in_2)

    arrive(loss_z)
    loss = functools.reduce(lambda a, b: a + b, [lz[i] for i in range(8)])
    loss_out[...] = loss / total_rows

    factor = 1.0 / math.sqrt(total_rows)
    arrive(out_4)
    og_out[...] = ag[1].astype(F32) * factor
    arrive(in_4)
    ig_out[...] = ag[0].astype(F32) * factor
    for copy in started:
        copy.wait_send()


def per_device(features, w_in, w_out, labels, pair_list):
    total_rows = lax.axis_size("pair") * lax.axis_size("shard") * features.shape[1]
    vmem = pl.BlockSpec(memory_space=pltpu.VMEM)
    smem = pl.BlockSpec(memory_space=pltpu.SMEM)
    hbm = pl.BlockSpec(memory_space=pltpu.HBM)
    w = WIDTH
    fg, ig, og, loss = pl.pallas_call(
        functools.partial(kernel, total_rows),
        name="contrastive_step",
        out_shape=(
            jax.ShapeDtypeStruct((128, w), BF16),
            jax.ShapeDtypeStruct((32, w), F32),
            jax.ShapeDtypeStruct((32, w), F32),
            jax.ShapeDtypeStruct((8, 128), F32),
        ),
        in_specs=[hbm, hbm, hbm, hbm, smem],
        out_specs=(vmem, vmem, vmem, vmem),
        scratch_shapes=[
            pltpu.VMEM((2, 4, 128, w), BF16),
            pltpu.VMEM((4, 4, 2, 32, w), BF16),
            pltpu.VMEM((4, 4, 2, 32, w), BF16),
            pltpu.VMEM((512, w), F32),
            pltpu.VMEM((w, w), BF16),
            pltpu.VMEM((w, w), F32),
            pltpu.VMEM((w, w), BF16),
            pltpu.VMEM((8, 128), jnp.int32),
            pltpu.VMEM((2, 8, 128), F32),
            pltpu.VMEM((128, w), F32),
            pltpu.VMEM((128, w), BF16),
            pltpu.VMEM((128, w), F32),
            pltpu.VMEM((2, 128, w), BF16),
            pltpu.VMEM((2, 4, 128, 256), BF16),
            pltpu.VMEM((2, 32, 32, 512), BF16),
            pltpu.VMEM((2, 4, 4, 2, 32, 256), BF16),
            pltpu.VMEM((2, 4, 4, 32, 256), BF16),
            pltpu.VMEM((2, 4, 4, 32, 256), BF16),
            pltpu.VMEM((2, 3, 4, 32, 256), BF16),
            pltpu.VMEM((2, 4, 32, 256), BF16),
            pltpu.VMEM((2, 8, 32, 256), BF16),
            pltpu.VMEM((2, 32, 256), BF16),
            pltpu.VMEM((2, 32, w), BF16),
            pltpu.VMEM((2, 8, 128), F32),
            pltpu.VMEM((4, 8, 128), F32),
            pltpu.VMEM((4, 8, 128), F32),
            pltpu.VMEM((8, 8, 128), F32),
            pltpu.SemaphoreType.DMA((COPIES,)),
            pltpu.SemaphoreType.DMA((COPIES,)),
            pltpu.SemaphoreType.DMA((4,)),
        ],
        compiler_params=pltpu.CompilerParams(
            collective_id=0, has_side_effects=True, vmem_limit_bytes=48 * 2**20
        ),
    )(features[0], w_in, w_out, labels, pair_list)
    return fg[None], ig, og, loss[0, 0]


def solution(mesh):
    in_specs = (
        P("pair", "shard", None),
        P("shard", None),
        P("shard", None),
        P(None, "shard"),
        P("shard", None),
    )
    out_specs = (P("pair", "shard", None), P("shard", None), P("shard", None), P())
    return jax.shard_map(
        per_device, mesh=mesh, in_specs=in_specs, out_specs=out_specs, check_vma=False
    )
```

time: 83.1 us -> 77.7 us (0.935)
  Pallas kernels: 75.7 us -> 69.7 us
    pallas_call x1, Pallas kernels: 75.7 us -> 69.7 us  [per_device(): pl.pallas_call(functools.partial(kernel, total_rows), name='contrastive_s...]
where the time goes in v3:
time: 77.7 us; the launch traced here: 76.9 us
  Pallas kernels  69.7 us (90%)
  local copies, waits for them, and re-layouts  6.51 us (8%)
    pallas_call x1, Pallas kernels, per_device(): pl.pallas_call(functools.partial(kernel, total_rows), name='contrastive_s...  69.7 us
    unnamed x14, local copies, waits for them, and re-layouts  6 us

profile of v3, /device:TPU:1, one launch (start us, length us, event | category | flops | bytes accessed | tf_op | source)
XLA Modules:
  0.0 76.9 jit_solution(978152397986526788)
XLA Ops:
  0.6 0.0 copy-start.4
  0.6 0.7 copy-done.4
  1.3 0.0 copy-start.3
  1.3 0.1 copy.9.pairs
  1.4 0.6 copy-done.3
  2.0 0.0 copy-start
  2.0 0.9 %copy-done = bf16[1,128,1024]{2,1,0:T(8,128)(2,1)S(1)} copy-done((bf16[1,128,1024]{2,1,0:T(8,128)(2,1)S(1)}, bf16[1,128,1024]{2,1,0:T(8,128)(2,1)}, u32[]{:S(2)}) %copy-start) | copy-done | bytes 262168
  2.9 0.0 copy-start.1
  3.0 0.8 %copy-done.1 = bf16[32,1024]{1,0:T(8,128)(2,1)S(1)} copy-done((bf16[32,1024]{1,0:T(8,128)(2,1)S(1)}, bf16[32,1024]{1,0:T(8,128)(2,1)}, u32[]{:S(2)}) %copy-start.1) | copy-done | bytes 65560
  3.8 0.0 copy-start.2
  3.8 0.8 %copy-done.2 = bf16[32,1024]{1,0:T(8,128)(2,1)S(1)} copy-done((bf16[32,1024]{1,0:T(8,128)(2,1)S(1)}, bf16[32,1024]{1,0:T(8,128)(2,1)}, u32[]{:S(2)}) %copy-start.2) | copy-done | bytes 65560
  4.6 69.7 %contrastive_step.1 = (bf16[128,1024]{1,0:T(8,128)(2,1)S(1)}, f32[32,1024]{1,0:T(8,128)S(1)}, f32[32,1024]{1,0:T(8,128)S(1)}, f32[8,128]{1,0:T(8,128)S(1)}) custom-call(bf16[128,1024]{1,0:T(8,128)(2,1)S(1)} %bitcast.3, bf16[32,1024]{1,0:T(8,128)(2,1)S(1)} %copy-done.1, bf16[32,1024]{1,0:T(8,128)(2,1)S(1)} %copy-done.2, s32[8,128]{1,0:T(8,128)S(1)} %copy-done.3, ...), custom_call_target="tpu_custom_call" | custom-call | tf_op jit(solution)/shard_map/contrastive_step/pallas_call | solution.py:449
  74.4 0.5 slice.3
  74.9 0.7 copy.13
  75.6 0.7 copy.14
  76.2 0.7 copy.15
Async XLA Ops:
  0.6 0.7 copy-start.4
  1.3 0.7 copy-start.3
  2.0 0.9 %copy-start = (bf16[1,128,1024]{2,1,0:T(8,128)(2,1)S(1)}, bf16[1,128,1024]{2,1,0:T(8,128)(2,1)}, u32[]{:S(2)}) copy-start(bf16[1,128,1024]{2,1,0:T(8,128)(2,1)} %param.5) | copy-start | bytes 786436
  2.9 0.8 %copy-start.1 = (bf16[32,1024]{1,0:T(8,128)(2,1)S(1)}, bf16[32,1024]{1,0:T(8,128)(2,1)}, u32[]{:S(2)}) copy-start(bf16[32,1024]{1,0:T(8,128)(2,1)} %w_in.1) | copy-start | bytes 196612
  3.8 0.8 %copy-start.2 = (bf16[32,1024]{1,0:T(8,128)(2,1)S(1)}, bf16[32,1024]{1,0:T(8,128)(2,1)}, u32[]{:S(2)}) copy-start(bf16[32,1024]{1,0:T(8,128)(2,1)} %w_out.1) | copy-start | bytes 196612

commit v4 on v3

--- a/solution.py
+++ b/solution.py
@@ -314,10 +314,10 @@
     turn(0, lambda b, cols: fx[zh, b, :, cols])
     pass_on(1, 2)
     arrive([from_core[0, j] for j in range(4)])
+    pass_on(1, 3)
     far_along_x(2)
+    far_along_x(3)
     hidden_near()
-    pass_on(1, 3)
-    far_along_x(3)
     for j in range(4):
         to_core(1, j)
     turn(1, lambda b, cols: hid[tile_at(b, 128), cols])
@@ -490,7 +490,7 @@
             pltpu.SemaphoreType.DMA((4,)),
         ],
         compiler_params=pltpu.CompilerParams(
-            collective_id=0, has_side_effects=True, vmem_limit_bytes=48 * 2**20
+            collective_id=0, has_side_effects=True, vmem_limit_bytes=54528 * 1024
         ),
     )(features[0], w_in, w_out, labels, pair_list)
     return fg[None], ig, og, loss[0, 0]

time: 77.7 us -> 76.3 us (0.982)
  local copies, waits for them, and re-layouts: 6.51 us -> 5.56 us
    unnamed x14 -> x12, local copies, waits for them, and re-layouts: 6 us -> 5.05 us
where the time goes in v4:
time: 76.3 us; the launch traced here: 76 us
  Pallas kernels  69.8 us (91%)
  local copies, waits for them, and re-layouts  5.56 us (7%)
    pallas_call x1, Pallas kernels, per_device(): pl.pallas_call(functools.partial(kernel, total_rows), name='contrastive_s...  69.8 us
    unnamed x12, local copies, waits for them, and re-layouts  5.05 us

profile of v4, /device:TPU:1, one launch (start us, length us, event | category | flops | bytes accessed | tf_op | source)
XLA Modules:
  0.0 76.0 jit_solution(12645860773132687041)
XLA Ops:
  0.6 0.0 copy-start.3
  0.6 0.7 copy-done.3
  1.3 0.0 copy-start.2
  1.3 0.1 copy.9.pairs
  1.4 0.6 copy-done.2
  2.0 0.0 copy-start
  2.0 0.8 %copy-done = bf16[32,1024]{1,0:T(8,128)(2,1)S(1)} copy-done((bf16[32,1024]{1,0:T(8,128)(2,1)S(1)}, bf16[32,1024]{1,0:T(8,128)(2,1)}, u32[]{:S(2)}) %copy-start) | copy-done | bytes 65560
  2.8 0.0 copy-start.1
  2.8 0.8 %copy-done.1 = bf16[32,1024]{1,0:T(8,128)(2,1)S(1)} copy-done((bf16[32,1024]{1,0:T(8,128)(2,1)S(1)}, bf16[32,1024]{1,0:T(8,128)(2,1)}, u32[]{:S(2)}) %copy-start.1) | copy-done | bytes 65560
  3.7 69.8 %contrastive_step.1 = (bf16[128,1024]{1,0:T(8,128)(2,1)S(1)}, f32[32,1024]{1,0:T(8,128)S(1)}, f32[32,1024]{1,0:T(8,128)S(1)}, f32[8,128]{1,0:T(8,128)S(1)}) custom-call(bf16[128,1024]{1,0:T(8,128)(2,1)} %bitcast.4, bf16[32,1024]{1,0:T(8,128)(2,1)S(1)} %copy-done, bf16[32,1024]{1,0:T(8,128)(2,1)S(1)} %copy-done.1, s32[8,128]{1,0:T(8,128)S(1)} %copy-done.2, ...), custom_call_target="tpu_custom_call" | custom-call | tf_op jit(solution)/shard_map/contrastive_step/pallas_call | solution.py:449
  73.5 0.5 slice.3
  74.0 0.7 copy.13
  74.7 0.7 copy.14
  75.4 0.7 copy.15
Async XLA Ops:
  0.6 0.7 copy-start.3
  1.3 0.7 copy-start.2
  2.0 0.8 %copy-start = (bf16[32,1024]{1,0:T(8,128)(2,1)S(1)}, bf16[32,1024]{1,0:T(8,128)(2,1)}, u32[]{:S(2)}) copy-start(bf16[32,1024]{1,0:T(8,128)(2,1)} %w_in.1) | copy-start | bytes 196612
  2.8 0.8 %copy-start.1 = (bf16[32,1024]{1,0:T(8,128)(2,1)S(1)}, bf16[32,1024]{1,0:T(8,128)(2,1)}, u32[]{:S(2)}) copy-start(bf16[32,1024]{1,0:T(8,128)(2,1)} %w_out.1) | copy-start | bytes 196612

commit v5 on v4

--- a/solution.py
+++ b/solution.py
@@ -53,8 +53,7 @@
     labels_hbm,
     pairs,
     fg_out,
-    ig_out,
-    og_out,
+    grads_out,
     loss_out,
     fx,
     wi,
@@ -250,7 +249,7 @@
     to_far(0)
     along_y(1, 0)
 
-    codes = [pairs[i, 0] * 8 + pairs[i, 1] for i in range(16)]
+    codes = [pairs[0, i] * 8 + pairs[1, i] for i in range(16)]
 
     def pair_weights(q):
         target = jnp.minimum(pair, q) * 8 + jnp.maximum(pair, q)
@@ -429,13 +428,12 @@
 
     arrive(loss_z)
     loss = functools.reduce(lambda a, b: a + b, [lz[i] for i in range(8)])
-    loss_out[...] = loss / total_rows
+    loss_out[...] = loss[0:1, 0:1] / total_rows
 
     factor = 1.0 / math.sqrt(total_rows)
     arrive(out_4)
-    og_out[...] = ag[1].astype(F32) * factor
     arrive(in_4)
-    ig_out[...] = ag[0].astype(F32) * factor
+    grads_out[...] = ag[...].astype(F32) * factor
     for copy in started:
         copy.wait_send()
 
@@ -446,17 +444,17 @@
     smem = pl.BlockSpec(memory_space=pltpu.SMEM)
     hbm = pl.BlockSpec(memory_space=pltpu.HBM)
     w = WIDTH
-    fg, ig, og, loss = pl.pallas_call(
+    inputs = (features[0], w_in, w_out, labels)
+    fg, grads, loss = pl.pallas_call(
         functools.partial(kernel, total_rows),
         name="contrastive_step",
         out_shape=(
             jax.ShapeDtypeStruct((128, w), BF16),
-            jax.ShapeDtypeStruct((32, w), F32),
-            jax.ShapeDtypeStruct((32, w), F32),
-            jax.ShapeDtypeStruct((8, 128), F32),
+            jax.ShapeDtypeStruct((2, 32, w), F32),
+            jax.ShapeDtypeStruct((1, 1), F32),
         ),
         in_specs=[hbm, hbm, hbm, hbm, smem],
-        out_specs=(vmem, vmem, vmem, vmem),
+        out_specs=(vmem, vmem, vmem),
         scratch_shapes=[
             pltpu.VMEM((2, 4, 128, w), BF16),
             pltpu.VMEM((4, 4, 2, 32, w), BF16),
@@ -490,10 +488,10 @@
             pltpu.SemaphoreType.DMA((4,)),
         ],
         compiler_params=pltpu.CompilerParams(
-            collective_id=0, has_side_effects=True, vmem_limit_bytes=54528 * 1024
+            collective_id=0, has_side_effects=True, vmem_limit_bytes=48 * 2**20
         ),
-    )(features[0], w_in, w_out, labels, pair_list)
-    return fg[None], ig, og, loss[0, 0]
+    )(*(pltpu.with_memory_space_constraint(a, pltpu.HBM) for a in inputs), pair_list.T)
+    return fg[None], grads[0], grads[1], loss.reshape(())
 
 
 def solution(mesh):

time: 76.3 us -> 74.9 us (0.982)
  local copies, waits for them, and re-layouts: 5.56 us -> 2.09 us
  between operations: 0.65 us -> 2.41 us
    unnamed x12 -> x3, local copies, waits for them, and re-layouts: 5.05 us -> 1.37 us
where the time goes in v5:
time: 74.9 us; the launch traced here: 74.8 us
  Pallas kernels  70.3 us (94%)
  between operations  2.41 us (3%)
  local copies, waits for them, and re-layouts  2.09 us (3%)
    pallas_call x1, Pallas kernels, per_device(): pl.pallas_call(functools.partial(kernel, total_rows), name='contrastive_s...  70.3 us

profile of v5, /device:TPU:1, one launch (start us, length us, event | category | flops | bytes accessed | tf_op | source)
XLA Modules:
  0.0 74.8 jit_solution(9063603168980429815)
XLA Ops:
  0.6 0.0 copy-start
  0.6 0.7 copy-done
  1.3 70.3 %contrastive_step.1 = (bf16[128,1024]{1,0:T(8,128)(2,1)S(1)}, f32[2,32,1024]{2,1,0:T(8,128)S(1)}, f32[1,1]{1,0:T(1,128)}) custom-call(bf16[128,1024]{1,0:T(8,128)(2,1)} %bitcast.10, bf16[32,1024]{1,0:T(8,128)(2,1)} %w_in.1, bf16[32,1024]{1,0:T(8,128)(2,1)} %w_out.1, s32[8,128]{1,0:T(8,128)} %labels_hbm.1, s32[2,16]{1,0:T(2,128)S(1)} %bitcast.9), custom_call_target="tpu_custom_call" | custom-call | tf_op jit(solution)/shard_map/contrastive_step/pallas_call | solution.py:448
  71.6 0.7 slice_bitcast_fusion
  72.4 0.7 copy.11
Async XLA Ops:
  0.6 0.7 copy-start

commit v6 on v5

--- a/solution.py
+++ b/solution.py
@@ -51,7 +51,7 @@
     w_in,
     w_out,
     labels_hbm,
-    pairs,
+    pairs_hbm,
     fg_out,
     grads_out,
     loss_out,
@@ -63,6 +63,7 @@
     emb,
     uni,
     labels,
+    pairs,
     ids,
     sign,
     slope,
@@ -125,6 +126,7 @@
         pltpu.make_async_copy(w_out, wo.at[zl, y, k], lsem.at[1]),
         pltpu.make_async_copy(feat, fx.at[zh, x], lsem.at[2]),
         pltpu.make_async_copy(labels_hbm, labels, lsem.at[3]),
+        pltpu.make_async_copy(pairs_hbm, pairs, lsem.at[4]),
     ]
     for copy in inputs:
         copy.start()
@@ -249,7 +251,6 @@
     to_far(0)
     along_y(1, 0)
 
-    codes = [pairs[0, i] * 8 + pairs[1, i] for i in range(16)]
 
     def pair_weights(q):
         target = jnp.minimum(pair, q) * 8 + jnp.maximum(pair, q)
@@ -261,6 +262,7 @@
 
     for copy in inputs:
         copy.wait()
+    codes = [pairs[0, i] * 8 + pairs[1, i] for i in range(16)]
     ids[0] = labels[...].astype(F32)
     ids[1] = pltpu.roll(ids[0], 64, 1)
     own_ids = jnp.broadcast_to(ids[0, pl.ds(pair, 1), :], (128, 128)).T
@@ -441,10 +443,9 @@
 def per_device(features, w_in, w_out, labels, pair_list):
     total_rows = lax.axis_size("pair") * lax.axis_size("shard") * features.shape[1]
     vmem = pl.BlockSpec(memory_space=pltpu.VMEM)
-    smem = pl.BlockSpec(memory_space=pltpu.SMEM)
     hbm = pl.BlockSpec(memory_space=pltpu.HBM)
     w = WIDTH
-    inputs = (features[0], w_in, w_out, labels)
+    inputs = (features[0], w_in, w_out, labels, pair_list.T)
     fg, grads, loss = pl.pallas_call(
         functools.partial(kernel, total_rows),
         name="contrastive_step",
@@ -453,7 +454,7 @@
             jax.ShapeDtypeStruct((2, 32, w), F32),
             jax.ShapeDtypeStruct((1, 1), F32),
         ),
-        in_specs=[hbm, hbm, hbm, hbm, smem],
+        in_specs=[hbm] * 5,
         out_specs=(vmem, vmem, vmem),
         scratch_shapes=[
             pltpu.VMEM((2, 4, 128, w), BF16),
@@ -464,6 +465,7 @@
             pltpu.VMEM((w, w), F32),
             pltpu.VMEM((w, w), BF16),
             pltpu.VMEM((8, 128), jnp.int32),
+            pltpu.SMEM((2, 16), jnp.int32),
             pltpu.VMEM((2, 8, 128), F32),
             pltpu.VMEM((128, w), F32),
             pltpu.VMEM((128, w), BF16),
@@ -485,12 +487,12 @@
             pltpu.VMEM((8, 8, 128), F32),
             pltpu.SemaphoreType.DMA((COPIES,)),
             pltpu.SemaphoreType.DMA((COPIES,)),
-            pltpu.SemaphoreType.DMA((4,)),
+            pltpu.SemaphoreType.DMA((5,)),
         ],
         compiler_params=pltpu.CompilerParams(
             collective_id=0, has_side_effects=True, vmem_limit_bytes=48 * 2**20
         ),
-    )(*(pltpu.with_memory_space_constraint(a, pltpu.HBM) for a in inputs), pair_list.T)
+    )(*(pltpu.with_memory_space_constraint(a, pltpu.HBM) for a in inputs))
     return fg[None], grads[0], grads[1], loss.reshape(())
 
 

time: 74.9 us -> 73.7 us (0.984)
  no operation moved by 1% of the time
where the time goes in v6:
time: 73.7 us; the launch traced here: 73.6 us
  Pallas kernels  69.8 us (95%)
  between operations  2.4 us (3%)
  local copies, waits for them, and re-layouts  1.42 us (2%)
    pallas_call x1, Pallas kernels, per_device(): pl.pallas_call(functools.partial(kernel, total_rows), name='contrastive_s...  69.8 us

profile of v6, /device:TPU:1, one launch (start us, length us, event | category | flops | bytes accessed | tf_op | source)
XLA Modules:
  0.0 73.6 jit_solution(15492950522615870244)
XLA Ops:
  0.6 69.8 %contrastive_step.1 = (bf16[128,1024]{1,0:T(8,128)(2,1)S(1)}, f32[2,32,1024]{2,1,0:T(8,128)S(1)}, f32[1,1]{1,0:T(1,128)}) custom-call(bf16[128,1024]{1,0:T(8,128)(2,1)} %bitcast.9, bf16[32,1024]{1,0:T(8,128)(2,1)} %w_in.1, bf16[32,1024]{1,0:T(8,128)(2,1)} %w_out.1, s32[8,128]{1,0:T(8,128)} %labels_hbm.1, s32[2,16]{1,0:T(2,128)} %bitcast.10), custom_call_target="tpu_custom_call" | custom-call | tf_op jit(solution)/shard_map/contrastive_step/pallas_call | solution.py:449
  70.4 0.7 slice_bitcast_fusion
  71.2 0.7 copy.11

commit v7 on v6

--- a/solution.py
+++ b/solution.py
@@ -128,9 +128,6 @@
         pltpu.make_async_copy(labels_hbm, labels, lsem.at[3]),
         pltpu.make_async_copy(pairs_hbm, pairs, lsem.at[4]),
     ]
-    for copy in inputs:
-        copy.start()
-
     barrier = pltpu.get_barrier_semaphore()
     partners = (
         [dict(dx=d) for d in (1, -1, 2)]
@@ -140,6 +137,8 @@
     )
     for offset in partners:
         pl.semaphore_signal(barrier, inc=1, device_id=device(**offset), device_id_type=MESH)
+    for copy in inputs:
+        copy.start()
     pl.semaphore_wait(barrier, len(partners))
 
     sources, held = (w_in, w_out), (wi, wo)

time: 73.7 us -> 73.7 us (level)
  no operation moved by 1% of the time
where the time goes in v7:
time: 73.7 us; the launch traced here: 73.6 us
  Pallas kernels  69.8 us (95%)
  between operations  2.4 us (3%)
  local copies, waits for them, and re-layouts  1.42 us (2%)
    pallas_call x1, Pallas kernels, per_device(): pl.pallas_call(functools.partial(kernel, total_rows), name='contrastive_s...  69.8 us

profile of v7, /device:TPU:1, one launch (start us, length us, event | category | flops | bytes accessed | tf_op | source)
XLA Modules:
  0.0 73.6 jit_solution(4400284794325833718)
XLA Ops:
  0.6 69.8 %contrastive_step.1 = (bf16[128,1024]{1,0:T(8,128)(2,1)S(1)}, f32[2,32,1024]{2,1,0:T(8,128)S(1)}, f32[1,1]{1,0:T(1,128)}) custom-call(bf16[128,1024]{1,0:T(8,128)(2,1)} %bitcast.9, bf16[32,1024]{1,0:T(8,128)(2,1)} %w_in.1, bf16[32,1024]{1,0:T(8,128)(2,1)} %w_out.1, s32[8,128]{1,0:T(8,128)} %labels_hbm.1, s32[2,16]{1,0:T(2,128)} %bitcast.10), custom_call_target="tpu_custom_call" | custom-call | tf_op jit(solution)/shard_map/contrastive_step/pallas_call | solution.py:448
  70.4 0.7 slice_bitcast_fusion
  71.1 0.7 copy.11
